TPU v7x, 128 devices: a whole 4x4x4 slice. The times are simulated.
128 devices in a mesh: section: 4 (over y), chain: 8 (over z, x_lo), tp: 4 (over x_hi, core).
Axes of the slice: x: 4 (x_hi: 2, x_lo: 2; x = x_hi * 2 + x_lo), y: 4, z: 4, core: 2. Of those that a mesh axis runs over, the one named last changes fastest.
Arguments:
- block_input: bfloat16 [8, 64, 8192], P('chain', None, 'tp'), may hold values from -6 to 6
- norm_gain: bfloat16 [8192], replicated, may hold values from 0.099609375 to 1.8984375
- w_query: bfloat16 [8192, 4096], P(('section', 'chain'), 'tp'), may hold values from -0.0625 to 0.0625
- w_kv: bfloat16 [8192, 2048], P(('section', 'chain'), 'tp'), may hold values from -0.0625 to 0.0625
- w_out: bfloat16 [4096, 8192], P('tp', ('section', 'chain')), may hold values from -0.09375 to 0.09375
- kv_cache: bfloat16 [4, 8, 256, 16, 2048], P('section', 'chain', None, None, 'tp'), may hold values from -6 to 6
- page_table: int32 [8, 256], P('chain'), may hold values from 0 to 255, each once within a row
- prefix_len: int32 [8], P('chain'), may hold values from 1024 to 4096, as said below
- page_owner: int32 [8, 16, 1], P('chain', 'section'), may hold values from 0 to 3; in each aligned block of 4 rows (0 to 3, 4 to 7, ..., all dimensions but the last counted through in order) at most 2 rows name the same one
Outputs:
- block_output: bfloat16 [4, 8, 64, 8192], P('section', 'chain', None, 'tp')
- decode_pool: bfloat16 [4, 8, 8, 16, 2048], P('section', 'chain', None, None, 'tp')
Inputs may be any that keep to these rules, and one draw needn't show every extreme that they name: `page_table`: each chain's table names every physical page once. `prefix_len`: some chain has a prefix of 4096 tokens. `page_owner`: among the 4 pages of one device, one owner is named at most 2 times.
All inputs are finite; a program needn't handle non-finite values.
Results may differ from a plain program's by a relative error of at most 0.02.
Values may be sent and summed in bfloat16 or wider, within the bound.
A program may use at most 128 MiB of HBM per device.

v0:
```python
import math

import jax
import jax.numpy as jnp
from jax import lax
from jax.sharding import PartitionSpec as P

HD = 128
SPAN = 32
PAGE = 16
SPANS = 2
PREFIX = 4096


def shifted(block, axis, distance):
    devices = range(lax.axis_size(axis))
    route = [(i - distance, i) for i in devices if i - distance in devices]
    return lax.ppermute(block, axis, route)


def rotate(values, positions):
    half_width = values.shape[-1] // 2
    inverse = 500000.0 ** (-(jnp.arange(half_width, dtype=jnp.float32) * 2.0 / values.shape[-1]))
    angles = positions[:, None] * inverse[None, :]
    cosine = jnp.cos(angles)[:, None, :]
    sine_of = jnp.sin(angles)[:, None, :]
    leading = values[..., :half_width]
    trailing = values[..., half_width:]
    return jnp.concatenate(
        [leading * cosine - trailing * sine_of, trailing * cosine + leading * sine_of], axis=-1
    )


def normalize(hidden, norm_gain):
    widened = hidden.astype(jnp.float32)
    scaled = widened * lax.rsqrt(jnp.mean(widened * widened, axis=-1, keepdims=True) + 1e-05)
    return (scaled * norm_gain.astype(jnp.float32)).astype(jnp.bfloat16)


def local(
    block_input, norm_gain, w_query, w_kv, w_out, kv_cache, page_table, prefix_len, page_owner
):
    sections = lax.axis_size("section")
    section_id = lax.axis_index("section")
    tp_id = lax.axis_index("tp")
    query_full, kv_full = (
        lax.all_gather(w_query, ("section", "chain"), axis=0, tiled=True),
        lax.all_gather(w_kv, ("section", "chain"), axis=0, tiled=True),
    )
    output_full = lax.all_gather(w_out, ("section", "chain"), axis=1, tiled=True)
    kv_width = kv_full.shape[1]
    kv_heads = kv_width // (2 * HD)
    group_size = query_full.shape[1] // HD // kv_heads
    scale_factor = 1.0 / math.sqrt(HD)
    length = prefix_len[0]
    cached = kv_cache[0, 0][page_table[0]].reshape(PREFIX, kv_heads, 2, HD)
    cached_keys = cached[:, :, 0]
    cached_values = cached[:, :, 1]
    local_input = block_input[0]
    new_rows = local_input.shape[0]
    share_cols = local_input.shape[1]
    local_input = lax.all_gather(local_input, "tp", axis=1, tiled=True)
    key_ids = jnp.arange(PREFIX + new_rows)

    def layer_mix(full_rows, row_start, kv_new):
        normed = normalize(full_rows, norm_gain)
        row_ids = row_start + jnp.arange(SPAN)
        positions = (length + row_ids).astype(jnp.float32)
        queries = jnp.dot(normed, query_full, preferred_element_type=jnp.float32).reshape(
            SPAN, -1, HD
        )
        queries = (
            rotate(queries, positions).astype(jnp.bfloat16).reshape(SPAN, kv_heads, group_size, HD)
        )
        projected = jnp.dot(normed, kv_full, preferred_element_type=jnp.float32).reshape(
            SPAN, kv_heads, 2, HD
        )
        fresh_keys = rotate(projected[:, :, 0], positions).astype(jnp.bfloat16)
        fresh_values = projected[:, :, 1].astype(jnp.bfloat16)
        fresh_rows = jnp.stack([fresh_keys, fresh_values], axis=2).reshape(SPAN, kv_width)
        kv_new = lax.dynamic_update_slice_in_dim(kv_new, fresh_rows, row_start, 0)
        recent = kv_new.reshape(new_rows, kv_heads, 2, HD)
        keys_all = jnp.concatenate([cached_keys, recent[:, :, 0]], axis=0)
        values_all = jnp.concatenate([cached_values, recent[:, :, 1]], axis=0)
        allowed = jnp.where(
            key_ids[None, :] < PREFIX,
            key_ids[None, :] < length,
            key_ids[None, :] - PREFIX <= row_ids[:, None],
        )
        scores = (
            jnp.einsum("rhgd,khd->hgrk", queries, keys_all, preferred_element_type=jnp.float32)
            * scale_factor
        )
        scores = jnp.where(allowed[None, None], scores, -1e30)
        row_peak = jnp.max(scores, axis=-1, keepdims=True)
        raised = jnp.exp(scores - row_peak)
        row_total = jnp.sum(raised, axis=-1, keepdims=True)
        weights = (raised / row_total).astype(jnp.bfloat16)
        mixed_rows = jnp.einsum(
            "hgrk,khd->rhgd", weights, values_all, preferred_element_type=jnp.float32
        )
        return (mixed_rows.astype(jnp.bfloat16).reshape(SPAN, -1), kv_new)

    def advance(step_id, carry):
        incoming, kv_new, collected = carry
        block_id = step_id - section_id
        is_live = (block_id >= 0) & (block_id < SPANS)
        row_start = jnp.clip(block_id, 0, SPANS - 1) * SPAN
        own_rows = lax.dynamic_slice_in_dim(local_input, row_start, SPAN, 0)
        current = jnp.where(section_id == 0, own_rows, incoming)
        mixed_rows, updated = layer_mix(current, row_start, kv_new)
        partial_sum = jnp.dot(mixed_rows, output_full, preferred_element_type=jnp.float32)
        summed = lax.psum(partial_sum.astype(jnp.bfloat16), "tp").astype(jnp.float32)
        result = (current.astype(jnp.float32) + summed).astype(jnp.bfloat16)
        kv_new = jnp.where(is_live, updated, kv_new)
        collected = jnp.where(
            is_live, lax.dynamic_update_slice_in_dim(collected, result, row_start, 0), collected
        )
        incoming = shifted(result, "section", 1)
        return (incoming, kv_new, collected)

    row_width = local_input.shape[1]
    start_carry = (
        jnp.zeros((SPAN, row_width), jnp.bfloat16),
        jnp.zeros((new_rows, kv_width), jnp.bfloat16),
        jnp.zeros((new_rows, row_width), jnp.bfloat16),
    )
    incoming, kv_new, collected = lax.fori_loop(0, SPANS + sections - 1, advance, start_carry)
    collected = lax.dynamic_slice_in_dim(collected, tp_id * share_cols, share_cols, 1)
    block_output = collected[None, None]
    page_count = new_rows // PAGE
    most_pages = max(2, (page_count + sections - 1) // sections)
    owners = page_owner[0, :, 0]
    page_ids = jnp.arange(page_count)
    earlier = (owners[:, None] == owners[None, :]) & (page_ids[None, :] < page_ids[:, None])
    page_ranks = jnp.sum(earlier.astype(jnp.int32), axis=1)
    slot_ids = owners * most_pages + page_ranks
    selection = (slot_ids[None, :] == jnp.arange(sections * most_pages)[:, None]).astype(
        jnp.bfloat16
    )
    placed = jnp.dot(
        selection, kv_new.reshape(page_count, PAGE * kv_width), preferred_element_type=jnp.float32
    )
    placed = placed.astype(jnp.bfloat16).reshape(sections, most_pages, PAGE, kv_width)
    pooled = lax.all_to_all(placed, "section", split_axis=0, concat_axis=0, tiled=True)
    return (block_output, pooled.reshape(1, 1, sections * most_pages, PAGE, kv_width))


def solution(mesh):
    in_specs = (
        P("chain", None, "tp"),
        P(),
        P(("section", "chain"), "tp"),
        P(("section", "chain"), "tp"),
        P("tp", ("section", "chain")),
        P("section", "chain", None, None, "tp"),
        P("chain", None),
        P("chain"),
        P("chain", "section", None),
    )
    out_specs = (P("section", "chain", None, "tp"), P("section", "chain", None, None, "tp"))
    return jax.shard_map(local, mesh=mesh, in_specs=in_specs, out_specs=out_specs, check_vma=False)
```

profile of v0, /device:TPU:25, one launch (start us, length us, event | category | flops | bytes accessed | tf_op | source)
XLA Modules:
  0.0 1414.5 jit_solution(8224553818663653772)
XLA Ops:
  23.3 9.0 fusion.33
  35.0 186.9 %all-gather.6.cloned.1.call-done = bf16[8192,512]{1,0:T(8,128)(2,1)} async-done(((bf16[256,512]{1,0:T(8,128)(2,1)}), bf16[8192,512]{1,0:T(8,128)(2,1)}) %all-gather.6.cloned.1.call-update) | async-done | bytes 8388624 | tf_op jit(solution)/shard_map/all_gather | solution.py:48
  221.9 363.1 %all-gather.8.cloned.1.call-done = bf16[8192,1024]{1,0:T(8,128)(2,1)} async-done(((bf16[256,1024]{1,0:T(8,128)(2,1)}), bf16[8192,1024]{1,0:T(8,128)(2,1)}) %all-gather.8.cloned.1.call-update) | async-done | bytes 16777232 | tf_op jit(solution)/shard_map/all_gather | solution.py:47
  584.9 360.5 %all-gather.10.cloned.1.call-done = bf16[1024,8192]{1,0:T(8,128)(2,1)} async-done(((bf16[1024,256]{1,0:T(8,128)(2,1)}), bf16[1024,8192]{1,0:T(8,128)(2,1)}) %all-gather.10.cloned.1.call-update) | async-done | bytes 16777232 | tf_op jit(solution)/shard_map/all_gather | solution.py:50
  945.6 453.4 %while.21 = (s32[]{:T(128)}, bf16[32,8192]{1,0:T(8,128)(2,1)S(1)}, bf16[64,512]{1,0:T(8,128)(2,1)S(1)}, bf16[64,8192]{1,0:T(8,128)(2,1)S(1)}, pred[]{:T(512)}, /...) while((s32[]{:T(128)}, bf16[32,8192]{1,0:T(8,128)(2,1)S(1)}, ...), condition=%wide.region_5.6_spmd.clone.clone, body=%wide.region_0.5_spmd.clone.clone.sunk | while | flops 1908144640 | bytes 94118728 | solution.py:128
  954.1 9.0 convolution_bitcast_fusion.2
  967.5 9.6 convolution_convert_fusion.3
  977.1 43.8 %all-reduce.2.cloned.1.call-done = bf16[32,8192]{1,0:T(8,128)(2,1)} async-done(((bf16[32,8192]{1,0:T(8,128)(2,1)}), bf16[32,8192]{1,0:T(8,128)(2,1)}) %all-reduce.2.cloned.1.call-update) | async-done | bytes 524304 | tf_op jit(solution)/shard_map/while/body/eval_jaxpr/psum | solution.py:113
  1023.5 13.9 collective-permute-done
  1059.3 9.6 convolution_convert_fusion.3
  1068.9 42.4 %all-reduce.2.cloned.1.call-done = bf16[32,8192]{1,0:T(8,128)(2,1)} async-done(((bf16[32,8192]{1,0:T(8,128)(2,1)}), bf16[32,8192]{1,0:T(8,128)(2,1)}) %all-reduce.2.cloned.1.call-update) | async-done | bytes 524304 | tf_op jit(solution)/shard_map/while/body/eval_jaxpr/psum | solution.py:113
  1113.9 13.9 collective-permute-done
  1136.3 9.0 convolution_bitcast_fusion.2
  1149.7 9.6 convolution_convert_fusion.3
  1159.3 42.4 %all-reduce.2.cloned.1.call-done = bf16[32,8192]{1,0:T(8,128)(2,1)} async-done(((bf16[32,8192]{1,0:T(8,128)(2,1)}), bf16[32,8192]{1,0:T(8,128)(2,1)}) %all-reduce.2.cloned.1.call-update) | async-done | bytes 524304 | tf_op jit(solution)/shard_map/while/body/eval_jaxpr/psum | solution.py:113
  1204.3 13.9 collective-permute-done
  1226.7 9.0 convolution_bitcast_fusion.2
  1240.1 9.6 convolution_convert_fusion.3
  1249.7 42.5 %all-reduce.2.cloned.1.call-done = bf16[32,8192]{1,0:T(8,128)(2,1)} async-done(((bf16[32,8192]{1,0:T(8,128)(2,1)}), bf16[32,8192]{1,0:T(8,128)(2,1)}) %all-reduce.2.cloned.1.call-update) | async-done | bytes 524304 | tf_op jit(solution)/shard_map/while/body/eval_jaxpr/psum | solution.py:113
  1294.7 13.9 collective-permute-done
  1317.1 9.0 convolution_bitcast_fusion.2
  1330.5 9.6 convolution_convert_fusion.3
  1340.1 42.4 %all-reduce.2.cloned.1.call-done = bf16[32,8192]{1,0:T(8,128)(2,1)} async-done(((bf16[32,8192]{1,0:T(8,128)(2,1)}), bf16[32,8192]{1,0:T(8,128)(2,1)}) %all-reduce.2.cloned.1.call-update) | async-done | bytes 524304 | tf_op jit(solution)/shard_map/while/body/eval_jaxpr/psum | solution.py:113
  1385.1 13.9 collective-permute-done
  (248 shorter events, 112.9 us)
Async XLA Ops:
  7.2 27.8 %all-gather.12.cloned.1.call-start = ((), (), s32[]{:S(2)}) async-start(), calls=%async_computation.4 | async-start | bytes 1310720 | tf_op jit(solution)/shard_map/all_gather | solution.py:62
  7.9 214.0 %all-gather.6.cloned.1.call-start = ((), (), s32[]{:S(2)}) async-start(), calls=%async_computation.1 | async-start | bytes 8650752 | tf_op jit(solution)/shard_map/all_gather | solution.py:48
  8.6 576.3 %all-gather.8.cloned.1.call-start = ((), (), s32[]{:S(2)}) async-start(), calls=%async_computation.2 | async-start | bytes 17301504 | tf_op jit(solution)/shard_map/all_gather | solution.py:47
  9.4 936.1 %all-gather.10.cloned.1.call-start = ((), (), s32[]{:S(2)}) async-start(), calls=%async_computation.3 | async-start | bytes 17301504 | tf_op jit(solution)/shard_map/all_gather | solution.py:50
  15.6 7.0 copy-start.4
  32.3 913.2 %copy-start.2 = (bf16[8192]{0:T(1024)(128)(2,1)S(1)}, bf16[8192]{0:T(1024)(128)(2,1)}, u32[]{:S(2)}) copy-start(bf16[8192]{0:T(1024)(128)(2,1)} %param.12) | copy-start | bytes 49156
  945.6 453.4 %copy-start.3 = (s32[4]{0:T(128)S(1)}, s32[4]{0:T(128)}, u32[]{:S(2)}) copy-start(s32[4]{0:T(128)} %multiply_add_fusion) | copy-start | bytes 52
  945.6 75.3 %all-reduce.2.cloned.1.call-start = ((), (), s32[]{:S(2)}) async-start(), calls=%async_computation.5 | async-start | bytes 1048576 | tf_op jit(solution)/shard_map/while/body/eval_jaxpr/psum | solution.py:113
  954.1 9.3 copy-start
  964.3 2.3 copy-start.1
  1022.2 15.3 %collective-permute-start = (bf16[32,8192]{1,0:T(8,128)(2,1)S(1)}, bf16[32,8192]{1,0:T(8,128)(2,1)S(1)}, u32[]{:S(2)}, u32[]{:S(2)}) collective-permute-start(bf16[32,8192]{1,0:T(8,128)(2,1)S(1)} %get-tuple-element.613), channel_id=1, source_target_pairs={{0,32},{32,64},{64,96},{1,33},{33,65},{65,97},{2,34},{34,66},{66,9... | collective-permute-start | bytes 1572872 | tf_op jit(solution)/shard_map/while/body/eval_jaxpr/ppermute | solution.py:18
  1037.4 73.9 %all-reduce.2.cloned.1.call-start = ((), (), s32[]{:S(2)}) async-start(), calls=%async_computation.5 | async-start | bytes 1048576 | tf_op jit(solution)/shard_map/while/body/eval_jaxpr/psum | solution.py:113
  1045.9 9.3 copy-start
  1112.6 15.3 %collective-permute-start = (bf16[32,8192]{1,0:T(8,128)(2,1)S(1)}, bf16[32,8192]{1,0:T(8,128)(2,1)S(1)}, u32[]{:S(2)}, u32[]{:S(2)}) collective-permute-start(bf16[32,8192]{1,0:T(8,128)(2,1)S(1)} %get-tuple-element.613), channel_id=1, source_target_pairs={{0,32},{32,64},{64,96},{1,33},{33,65},{65,97},{2,34},{34,66},{66,9... | collective-permute-start | bytes 1572872 | tf_op jit(solution)/shard_map/while/body/eval_jaxpr/ppermute | solution.py:18
  1127.8 73.9 %all-reduce.2.cloned.1.call-start = ((), (), s32[]{:S(2)}) async-start(), calls=%async_computation.5 | async-start | bytes 1048576 | tf_op jit(solution)/shard_map/while/body/eval_jaxpr/psum | solution.py:113
  1136.3 9.3 copy-start
  1203.0 15.3 %collective-permute-start = (bf16[32,8192]{1,0:T(8,128)(2,1)S(1)}, bf16[32,8192]{1,0:T(8,128)(2,1)S(1)}, u32[]{:S(2)}, u32[]{:S(2)}) collective-permute-start(bf16[32,8192]{1,0:T(8,128)(2,1)S(1)} %get-tuple-element.613), channel_id=1, source_target_pairs={{0,32},{32,64},{64,96},{1,33},{33,65},{65,97},{2,34},{34,66},{66,9... | collective-permute-start | bytes 1572872 | tf_op jit(solution)/shard_map/while/body/eval_jaxpr/ppermute | solution.py:18
  1218.2 73.9 %all-reduce.2.cloned.1.call-start = ((), (), s32[]{:S(2)}) async-start(), calls=%async_computation.5 | async-start | bytes 1048576 | tf_op jit(solution)/shard_map/while/body/eval_jaxpr/psum | solution.py:113
  1226.7 9.3 copy-start
  1293.4 15.3 %collective-permute-start = (bf16[32,8192]{1,0:T(8,128)(2,1)S(1)}, bf16[32,8192]{1,0:T(8,128)(2,1)S(1)}, u32[]{:S(2)}, u32[]{:S(2)}) collective-permute-start(bf16[32,8192]{1,0:T(8,128)(2,1)S(1)} %get-tuple-element.613), channel_id=1, source_target_pairs={{0,32},{32,64},{64,96},{1,33},{33,65},{65,97},{2,34},{34,66},{66,9... | collective-permute-start | bytes 1572872 | tf_op jit(solution)/shard_map/while/body/eval_jaxpr/ppermute | solution.py:18
  1308.7 73.8 %all-reduce.2.cloned.1.call-start = ((), (), s32[]{:S(2)}) async-start(), calls=%async_computation.5 | async-start | bytes 1048576 | tf_op jit(solution)/shard_map/while/body/eval_jaxpr/psum | solution.py:113
  1317.1 9.3 copy-start
  1383.7 15.3 %collective-permute-start = (bf16[32,8192]{1,0:T(8,128)(2,1)S(1)}, bf16[32,8192]{1,0:T(8,128)(2,1)S(1)}, u32[]{:S(2)}, u32[]{:S(2)}) collective-permute-start(bf16[32,8192]{1,0:T(8,128)(2,1)S(1)} %get-tuple-element.613), channel_id=1, source_target_pairs={{0,32},{32,64},{64,96},{1,33},{33,65},{65,97},{2,34},{34,66},{66,9... | collective-permute-start | bytes 1572872 | tf_op jit(solution)/shard_map/while/body/eval_jaxpr/ppermute | solution.py:18
  1399.9 7.4 all-to-all-start
  (4 other events, 9.0 us)
Sparse Core Ops, SparseCore 0:
  9.7 23.2 all-gather.11
  34.6 187.2 all-gather.5
  223.5 361.3 all-gather.7
  586.4 359.0 all-gather.9
  977.2 43.6 all-reduce.1
  1069.0 42.2 all-reduce.1
  1159.4 42.2 all-reduce.1
  1249.8 42.2 all-reduce.1
  1340.2 42.2 all-reduce.1
where the time goes:
time: 1420 us; the launch traced here: 1410 us
  waiting for transfers between devices  1200 us (85%)
  matrix products  126 us (9%)
  other arithmetic  35.5 us (2%)
  local copies, waits for them, and re-layouts  28 us (2%)
    all_gather x1, waiting for transfers between devices, local(): lax.all_gather(w_query, ('section', 'chain'), axis=0, tiled=True)  363 us
    all_gather x1, waiting for transfers between devices, local(): lax.all_gather(w_out, ('section', 'chain'), axis=1, tiled=True)  361 us
    psum x5, waiting for transfers between devices, advance(): lax.psum(partial_sum.astype(jnp.bfloat16), 'tp').astype(jnp.float32)  213 us
    all_gather x1, waiting for transfers between devices, local(): lax.all_gather(w_kv, ('section', 'chain'), axis=0, tiled=True)  187 us
    ppermute x5, waiting for transfers between devices, shifted(): return lax.ppermute(block, axis, route)  69.6 us
    dot_general x5, matrix products, advance(): jnp.dot(mixed_rows, output_full, preferred_element_type=jnp.float32)  47.8 us
    dot_general x5, matrix products, layer_mix(): jnp.dot(normed, query_full, preferred_element_type=jnp.float32)  44.8 us
  transfers between devices with their start and end apart: 15, of which 14 were waited for; matrix products, arithmetic and copies ran while one was open for 2% of the time, Pallas kernels for 0%

commit v1 on v0

v1 whole, which is shorter than its diff:
```python
import math

import jax
import jax.numpy as jnp
from jax import lax
from jax.experimental import pallas as pl
from jax.experimental.pallas import tpu as pltpu
from jax.sharding import PartitionSpec as P

HD = 128
PAGE = 16
PREFIX = 4096
NEW = 64
WIDTH = 8192
NSEC = 4
NCH = 8
NTP = 4
QC = 256
PC = 384
CH = 512
NCHUNK = PREFIX // CH
STREAMS = ((0, 32), (32, 32))
NS = len(STREAMS)
R = STREAMS[0][1]
MESH = pl.DeviceIdType.MESH
BF = jnp.bfloat16
F32 = jnp.float32


def kernel(
    hin, wsend, wo, cache, bias, cosd, sind, sel,
    bout, pool,
    cachev, wq_l, wo_l, h0, hA, part1, rbuf, ssend, srecv, sbuf2, qbuf, kvnew, S, msend, mixb, osend, ob, placed, obuf, pbuf,
    csem, h0s, h0r, h2s, h2r, wqs, wqr, wos, wor,
    s1, r1, ss_s, ss_r, s2, r2, s3, r3, s4, r4, s5, r5, s6, r6, s7, r7, s7f, r7f, so, ro, ps, pr,
):
    y = lax.axis_index("section")
    c = lax.axis_index("chain")
    t = lax.axis_index("tp")
    u = t // 2
    k = t % 2
    own = 2 * y + u
    twin = (y, c, 2 * u + 1 - k)

    def remote(src, dst, ssem, rsem, dev):
        return pltpu.make_async_remote_copy(
            src_ref=src, dst_ref=dst, send_sem=ssem, recv_sem=rsem, device_id=dev, device_id_type=MESH
        )

    def got(dst, rsem):
        pltpu.make_async_copy(dst, dst, rsem).wait()

    barrier = pltpu.get_barrier_semaphore()
    for d in range(1, NCH):
        pl.semaphore_signal(barrier, inc=1, device_id=(y, (c + d) % NCH, t), device_id_type=MESH)
    for dy in range(NSEC):
        for dt in range(NTP):
            if dy or dt:
                pl.semaphore_signal(
                    barrier, inc=1, device_id=((y + dy) % NSEC, c, (t + dt) % NTP), device_id_type=MESH
                )
    pl.semaphore_wait(barrier, NCH - 1 + NSEC * NTP - 1)

    def first_hop(d):
        peer = (c + d) % NCH
        src = hin.at[:, pl.ds(pl.multiple_of(peer * QC, QC), QC)]
        return lambda: remote(src, h0.at[c % 2], h0s.at[d], h0r.at[c % 2], (y, peer, t)), src

    @pl.when(c // 2 == y)
    def _():
        for d in range(1, NCH):
            first_hop(d)[0]().start()
        pltpu.make_async_copy(first_hop(0)[1], h0.at[c % 2], h0r.at[c % 2]).start()

    def wq_copy(d):
        peer = (y + d) % NSEC
        return remote(wsend.at[peer], wq_l.at[y], wqs.at[d], wqr.at[y], (peer, c, t))

    for d in range(1, NSEC):
        wq_copy(d).start()
    pltpu.make_async_copy(wsend.at[y], wq_l.at[y], wqr.at[y]).start()

    def wo_copy(d):
        peer = (y + d) % NSEC
        src = wo.at[pl.ds(pl.multiple_of(peer * QC, QC), QC), :]
        return lambda: remote(src, wo_l.at[k, y % 2], wos.at[d], wor.at[k, y % 2], (peer, c, 2 * u + y // 2)), src

    cache_copy = pltpu.make_async_copy(cache, cachev, csem)

    def second_hop(j, st):
        r0 = STREAMS[st][0]
        src = h0.at[j, pl.ds(r0, R), :]
        dst = hA.at[st, t // 2, 2 * y + j, :, pl.ds(pl.multiple_of((t % 2) * QC, QC), QC)]
        rsem = h2r.at[st, t % 2]
        return lambda: remote(src, dst, h2s.at[st, j], rsem, (y, c, 2 * j + t // 2)), src, dst, rsem

    for j in range(2):
        got(h0.at[j], h0r.at[j])
    for st in range(NS):
        for j in range(2):
            mine = (j == u) & (k == t // 2)

            @pl.when(mine)
            def _():
                _, src, dst, rsem = second_hop(j, st)
                pltpu.make_async_copy(src, dst, rsem).start()

            @pl.when(jnp.logical_not(mine))
            def _():
                second_hop(j, st)[0]().start()

    def ag_copy(st, e):
        g = (own + e) % 8
        piece = hA.at[st, k, own]
        return remote(piece, piece, s7.at[st, e], r7.at[st, own], (g // 2, c, 2 * (g % 2) + k))

    def twin_copy(st, e):
        g = (own + 8 - e) % 8
        piece = hA.at[st, k, g]
        return remote(piece, piece, s7f.at[st, e], r7f.at[st, g], twin)

    def ag_send(st):
        for e in range(1, 8):
            ag_copy(st, e).start()
        twin_copy(st, 0).start()

    def ag_forward(st):
        for e in range(1, 8):
            g = (own + 8 - e) % 8
            got(hA.at[st, k, g], r7.at[st, g])
            twin_copy(st, e).start()

    def ag_wait(st):
        for e in range(8):
            g = (own + 8 - e) % 8
            got(hA.at[st, 1 - k, g], r7f.at[st, g])

    def ag_sent(st):
        for e in range(1, 8):
            ag_copy(st, e).wait_send()
        for e in range(8):
            twin_copy(st, e).wait_send()

    for st in range(NS):
        for a in range(2):
            got(hA.at[st, k, own, :, pl.ds(a * QC, QC)], h2r.at[st, a])
        ag_send(st)

    for d in range(NSEC):
        if d:
            wo_copy(d)[0]().start()
        else:
            @pl.when(k == y // 2)
            def _():
                pltpu.make_async_copy(wo_copy(0)[1], wo_l.at[k, y % 2], wor.at[k, y % 2]).start()

            @pl.when(k != y // 2)
            def _():
                wo_copy(0)[0]().start()
    cache_copy.start()

    @pl.when(c // 2 == y)
    def _():
        for d in range(1, NCH):
            first_hop(d)[0]().wait_send()

    for st in range(NS):
        for j in range(2):
            mine = (j == u) & (k == t // 2)

            @pl.when(jnp.logical_not(mine))
            def _():
                second_hop(j, st)[0]().wait_send()

    for st in range(NS):
        ag_forward(st)
    for d in range(NSEC):
        got(wq_l.at[d], wqr.at[d])
    for d in range(1, NSEC):
        wq_copy(d).wait_send()
    for st in range(NS):
        ag_wait(st)
    for a in range(2):
        for b in range(2):
            got(wo_l.at[a, b], wor.at[a, b])
    for d in range(NSEC):
        if d:
            wo_copy(d)[0]().wait_send()
        else:
            @pl.when(k != y // 2)
            def _():
                wo_copy(0)[0]().wait_send()
    cache_copy.wait()

    def p1_copy(st, d):
        peer = (c + d) % NCH
        return remote(part1.at[st, peer], rbuf.at[st, c], s1.at[st, d], r1.at[st, c], (y, peer, t))

    def ss_copy(st, d):
        peer = (c + d) % NCH
        return remote(ssend.at[st, peer], srecv.at[st, c], ss_s.at[st, d], ss_r.at[st, c], (y, peer, t))

    def project(st):
        total = None
        for half in range(2):
            x = hA[st, half].reshape(NCH * R, 512)
            w = wq_l[pl.ds(2 * half, 2)].reshape(512, PC)
            term = jnp.dot(x, w, preferred_element_type=F32)
            total = term if total is None else total + term
        part1[st] = total.astype(BF).reshape(NCH, R, PC)
        for d in range(1, NCH):
            p1_copy(st, d).start()
        ones = jnp.ones((8, 128), BF)
        for g in range(NCH):
            acc = None
            for half in range(2):
                wide = hA[st, half, g].astype(F32)
                square = wide * wide
                for a in range(4):
                    piece = square[:, a * 128:(a + 1) * 128]
                    acc = piece if acc is None else acc + piece
            high = acc.astype(BF)
            low = (acc - high.astype(F32)).astype(BF)
            dims = (((1,), (1,)), ((), ()))
            row = lax.dot_general(ones, high, dims, preferred_element_type=F32)
            row = row + lax.dot_general(ones, low, dims, preferred_element_type=F32)
            ssend[st, g] = jnp.concatenate([row, jnp.zeros((8, 128 - R), F32)], axis=1)
        for d in range(1, NCH):
            ss_copy(st, d).start()
        rbuf[st, c] = part1[st, c]
        srecv[st, c] = ssend[st, c]

    def p2_copy(st, s):
        return remote(sbuf2.at[st], qbuf.at[st, y], s2.at[st], r2.at[st, y], (s, c, t))

    def finish_projection(st, s):
        r0 = STREAMS[st][0]
        for d in range(1, NCH):
            g = (c + NCH - d) % NCH
            got(rbuf.at[st, g], r1.at[st, g])
            got(srecv.at[st, g], ss_r.at[st, g])
        total = rbuf[st, 0].astype(F32)
        squares = srecv[st, 0]
        for g in range(1, NCH):
            total = total + rbuf[st, g].astype(F32)
            squares = squares + srecv[st, g]
        inv = lax.rsqrt(squares * (1.0 / WIDTH) + 1e-05)[0:1, :R]
        eye = lax.broadcasted_iota(jnp.int32, (R, R), 0) == lax.broadcasted_iota(jnp.int32, (R, R), 1)
        scale = jnp.sum(jnp.where(eye, inv, 0.0), axis=1, keepdims=True)
        total = total * scale
        cs = cosd[r0:r0 + R, :]
        sn = sind[r0:r0 + R, :]
        to_score = math.log2(math.e) / math.sqrt(HD)

        def rope(v):
            return v * cs + pltpu.roll(v, 64, 1) * sn

        q0 = rope(total[:, 0:128]) * to_score
        q1 = rope(total[:, 128:256]) * to_score
        kv = total[:, 256:384]
        even = (y % 2 == 0).astype(F32)
        kv = rope(kv) * even + kv * (1.0 - even)
        sbuf2[st] = jnp.concatenate([q0, q1, kv], axis=1).astype(BF)

        @pl.when(y == s)
        def _():
            qbuf[st, y] = sbuf2[st]

        @pl.when(y != s)
        def _():
            p2_copy(st, s).start()

        for d in range(1, NCH):
            p1_copy(st, d).wait_send()
            ss_copy(st, d).wait_send()
        ag_sent(st)

        @pl.when((s > 0) & (y == s - 1))
        def _():
            bout_sent(st)

    def p3_copy(st, d):
        peer = (y + d) % NSEC
        return remote(msend.at[st, peer], mixb.at[st, k, c], s3.at[st, d], r3.at[st], (peer, c, t))

    def pool_copy(d):
        peer = (y + d) % NSEC
        return remote(placed.at[peer], pbuf.at[y], ps.at[d], pr.at[y], (peer, c, t))

    def attend(st):
        r0 = STREAMS[st][0]
        seen = r0 + R
        for d in range(1, NSEC):
            g = (y + d) % NSEC
            got(qbuf.at[st, g], r2.at[st, g])
        for g in range(NSEC):
            kvnew[r0:r0 + R, g * 128:(g + 1) * 128] = qbuf[st, g, :, QC:PC]
        dims = (((1,), (1,)), ((), ()))
        for j in range(2):
            q = jnp.concatenate(
                [qbuf[st, 2 * j + hh // 2, :, (hh % 2) * 128:(hh % 2 + 1) * 128] for hh in range(4)], axis=0
            )
            kcol = j * 256
            vcol = j * 256 + 128
            sf = lax.dot_general(q, kvnew[0:seen, kcol:kcol + 128], dims, preferred_element_type=F32)
            row = lax.broadcasted_iota(jnp.int32, (4, R, seen), 1).reshape(4 * R, seen) + r0
            col = lax.broadcasted_iota(jnp.int32, (4 * R, seen), 1)
            sf = jnp.where(col <= row, sf, -1e30)

            def scores(i, peak):
                keys = cachev[pl.ds(pl.multiple_of(i * CH, CH), CH), kcol:kcol + 128]
                sc = lax.dot_general(q, keys, dims, preferred_element_type=F32) + bias[pl.ds(i, 1), :]
                S[i] = sc
                for a in range(CH // 128):
                    peak = jnp.maximum(peak, sc[:, a * 128:(a + 1) * 128])
                return peak

            peak = lax.fori_loop(0, NCHUNK, scores, jnp.full((4 * R, 128), -1e30, F32))
            top = jnp.maximum(jnp.max(peak, axis=1, keepdims=True), jnp.max(sf, axis=1, keepdims=True))

            pf = jnp.exp2(sf - top)
            acc0 = jnp.dot(pf.astype(BF), kvnew[0:seen, vcol:vcol + 128], preferred_element_type=F32)

            def weigh(i, carry):
                acc, den = carry
                p = jnp.exp2(S[i] - top)
                for a in range(CH // 128):
                    den = den + p[:, a * 128:(a + 1) * 128]
                values = cachev[pl.ds(pl.multiple_of(i * CH, CH), CH), vcol:vcol + 128]
                return acc + jnp.dot(p.astype(BF), values, preferred_element_type=F32), den

            acc, den = lax.fori_loop(0, NCHUNK, weigh, (acc0, jnp.zeros((4 * R, 128), F32)))
            den = jnp.sum(den, axis=1, keepdims=True) + jnp.sum(pf, axis=1, keepdims=True)
            mixed = (acc / den).astype(BF)
            for hh in range(4):
                msend[st, 2 * j + hh // 2, :, (hh % 2) * 128:(hh % 2 + 1) * 128] = mixed[hh * R:(hh + 1) * R]
        for d in range(1, NSEC):
            p3_copy(st, d).start()
        mixb[st, k, c] = msend[st, y]

    def place_pages():
        for slot in range(2 * NSEC):
            acc = None
            for q in range(NEW // PAGE):
                term = kvnew[q * PAGE:(q + 1) * PAGE, :].astype(F32) * sel[slot, q]
                acc = term if acc is None else acc + term
            placed[slot // 2, (slot % 2) * PAGE:(slot % 2 + 1) * PAGE, :] = acc.astype(BF)
        for d in range(1, NSEC):
            pool_copy(d).start()
        pbuf[y] = placed[y]

    def mix(st, s):
        @pl.when(y == s)
        def _():
            attend(st)
            if st == NS - 1:
                place_pages()

        @pl.when(y != s)
        def _():
            p2_copy(st, s).wait_send()

    def p4_copy(st, d):
        peer = (c + d) % NCH
        piece = mixb.at[st, k, c]
        return remote(piece, piece, s4.at[st, d], r4.at[st, c], (y, peer, t))

    def p5_copy(st, d):
        g = (c + NCH - d) % NCH
        piece = mixb.at[st, k, g]
        return remote(piece, piece, s5.at[st, d], r5.at[st, g], twin)

    def spread(st, s):
        @pl.when(y != s)
        def _():
            got(mixb.at[st, k, c], r3.at[st])

        for d in range(1, NCH):
            p4_copy(st, d).start()
        p5_copy(st, 0).start()

    def spread_twin(st):
        for d in range(1, NCH):
            g = (c + NCH - d) % NCH
            got(mixb.at[st, k, g], r4.at[st, g])
            p5_copy(st, d).start()

    def p6_copy(st, e):
        g = (own + e) % 8
        return remote(osend.at[st, g], ob.at[st, own], s6.at[st, e], r6.at[st, own], (g // 2, c, 2 * (g % 2) + k))

    def bout_copy(st, d):
        r0 = STREAMS[st][0]
        peer = (c + d) % NCH
        src = hA.at[st, t // 2, peer, :, pl.ds(pl.multiple_of((t % 2) * QC, QC), QC)]
        dst = obuf.at[c, pl.ds(r0, R), :]
        return lambda: remote(src, dst, so.at[st, d], ro.at[st, c], (y, peer, t)), src, dst

    def bout_sent(st):
        for d in range(1, NCH):
            bout_copy(st, d)[0]().wait_send()
        got(bout_copy(st, 0)[2], so.at[st, 0])

    def output_projection(st, s):
        for d in range(NCH):
            g = (c + NCH - d) % NCH
            got(mixb.at[st, 1 - k, g], r5.at[st, g])
        for b in range(2):
            total = None
            for a in range(2):
                x = mixb[st, a].reshape(NCH * R, QC)
                term = jnp.dot(x, wo_l[a, b], preferred_element_type=F32)
                total = term if total is None else total + term
            osend[st, :, :, b * QC:(b + 1) * QC] = total.astype(BF).reshape(NCH, R, QC)

        for d in range(1, NCH):
            p4_copy(st, d).wait_send()
        for d in range(NCH):
            p5_copy(st, d).wait_send()

        @pl.when(y == s)
        def _():
            for d in range(1, NSEC):
                p3_copy(st, d).wait_send()

        for e in range(1, 8):
            p6_copy(st, e).start()
        ob[st, own] = osend[st, own]

    def residual(st):
        for e in range(1, 8):
            g = (own + 8 - e) % 8
            got(ob.at[st, g], r6.at[st, g])
        total = ob[st, 0].astype(F32)
        for g in range(1, 8):
            total = total + ob[st, g].astype(F32)
        hA[st, k, own] = (hA[st, k, own].astype(F32) + total).astype(BF)
        ag_send(st)
        for e in range(1, 8):
            p6_copy(st, e).wait_send()

    def put_out(st, s):
        @pl.when(y == s)
        def _():
            for d in range(1, NCH):
                bout_copy(st, d)[0]().start()
            _, src, dst = bout_copy(st, 0)
            pltpu.make_async_copy(src, dst, so.at[st, 0]).start()

    def section_step(s, carry):
        for st in range(NS):
            project(st)
        for st in range(NS):
            finish_projection(st, s)
        for st in range(NS):
            mix(st, s)
            spread(st, s)
        for st in range(NS):
            spread_twin(st)
        for st in range(NS):
            output_projection(st, s)
        for st in range(NS):
            residual(st)
        for st in range(NS):
            ag_forward(st)
        for st in range(NS):
            ag_wait(st)
            put_out(st, s)
        return carry

    lax.fori_loop(0, NSEC, section_step, 0)

    for st in range(NS):
        ag_sent(st)

        @pl.when(y == NSEC - 1)
        def _():
            bout_sent(st)

        for d in range(1, NCH):
            g = (c + NCH - d) % NCH
            got(obuf.at[g, pl.ds(STREAMS[st][0], R), :], ro.at[st, g])
    for d in range(1, NSEC):
        g = (y + NSEC - d) % NSEC
        got(pbuf.at[g], pr.at[g])
        pool_copy(d).wait_send()
    for g in range(NCH):
        bout[:, g * QC:(g + 1) * QC] = obuf[g]
    for g in range(NSEC):
        pool[g] = pbuf[g]


def local(block_input, norm_gain, w_query, w_kv, w_out, kv_cache, page_table, prefix_len, page_owner):
    y = lax.axis_index("section")
    c = lax.axis_index("chain")
    length = prefix_len[0]
    rows = w_query.shape[0]
    gain = lax.dynamic_slice_in_dim(norm_gain, (y * NCH + c) * rows, rows, 0).astype(F32)[:, None]
    wq = (w_query.astype(F32) * gain).astype(BF).reshape(rows, NSEC, QC)
    wkv = (w_kv.astype(F32) * gain).astype(BF).reshape(rows, NSEC, PC - QC)
    wsend = jnp.concatenate([wq, wkv], axis=-1).transpose(1, 0, 2)

    pages = PREFIX // PAGE
    ids = jnp.arange(pages, dtype=jnp.int32)
    logical = jnp.sum(jnp.where(page_table[0][None, :] == ids[:, None], ids[None, :], 0), axis=1)
    place = logical[:, None] * PAGE + jnp.arange(PAGE, dtype=jnp.int32)[None, :]
    bias = jnp.where(place < length, 0.0, -1e30).astype(F32).reshape(NCHUNK, CH)

    inverse = 500000.0 ** (-(jnp.arange(HD // 2, dtype=F32) * 2.0 / HD))
    angles = (length + jnp.arange(NEW)).astype(F32)[:, None] * inverse[None, :]
    cosine, sine = jnp.cos(angles), jnp.sin(angles)
    cosd = jnp.concatenate([cosine, cosine], axis=1)
    sind = jnp.concatenate([-sine, sine], axis=1)

    owners = page_owner[0, :, 0]
    q = jnp.arange(NEW // PAGE)
    earlier = (owners[:, None] == owners[None, :]) & (q[None, :] < q[:, None])
    slots = owners * 2 + jnp.sum(earlier.astype(jnp.int32), axis=1)
    sel = (slots[None, :] == jnp.arange(2 * NSEC)[:, None]).astype(F32)

    vm = pl.BlockSpec(memory_space=pltpu.VMEM)
    dma = pltpu.SemaphoreType.DMA
    V = pltpu.VMEM
    bout, pool = pl.pallas_call(
        kernel,
        out_shape=(
            jax.ShapeDtypeStruct((NEW, WIDTH // NTP), BF),
            jax.ShapeDtypeStruct((NSEC, 2 * PAGE, 512), BF),
        ),
        in_specs=[vm, vm, vm, pl.BlockSpec(memory_space=pl.ANY), vm, vm, vm, pl.BlockSpec(memory_space=pltpu.SMEM)],
        out_specs=(vm, vm),
        scratch_shapes=[
            V((PREFIX, 512), BF),
            V((NSEC, 256, PC), BF),
            V((2, 2, 256, 256), BF),
            V((2, NEW, QC), BF),
            V((NS, 2, NCH, R, 512), BF),
            V((NS, NCH, R, PC), BF),
            V((NS, NCH, R, PC), BF),
            V((NS, NCH, 8, 128), F32),
            V((NS, NCH, 8, 128), F32),
            V((NS, R, PC), BF),
            V((NS, NSEC, R, PC), BF),
            V((NEW, 512), BF),
            V((NCHUNK, 4 * R, CH), F32),
            V((NS, NSEC, R, QC), BF),
            V((NS, 2, NCH, R, QC), BF),
            V((NS, NCH, R, 512), BF),
            V((NS, NCH, R, 512), BF),
            V((NSEC, 2 * PAGE, 512), BF),
            V((NCH, NEW, QC), BF),
            V((NSEC, 2 * PAGE, 512), BF),
            dma(()),
            dma((NCH,)), dma((2,)),
            dma((NS, 2)), dma((NS, 2)),
            dma((NSEC,)), dma((NSEC,)),
            dma((NSEC,)), dma((2, 2)),
            dma((NS, NCH)), dma((NS, NCH)),
            dma((NS, NCH)), dma((NS, NCH)),
            dma((NS,)), dma((NS, NSEC)),
            dma((NS, NSEC)), dma((NS,)),
            dma((NS, NCH)), dma((NS, NCH)),
            dma((NS, NCH)), dma((NS, NCH)),
            dma((NS, 8)), dma((NS, 8)),
            dma((NS, 8)), dma((NS, 8)),
            dma((NS, 8)), dma((NS, 8)),
            dma((NS, NCH)), dma((NS, NCH)),
            dma((NSEC,)), dma((NSEC,)),
        ],
        compiler_params=pltpu.CompilerParams(
            collective_id=0, has_side_effects=True, vmem_limit_bytes=48 * 1024 * 1024
        ),
    )(block_input[0], wsend, w_out, kv_cache.reshape(PREFIX, 512), bias, cosd, sind, sel)
    return bout[None, None], pool.reshape(1, 1, 2 * NSEC, PAGE, 512)


def solution(mesh):
    in_specs = (
        P("chain", None, "tp"),
        P(),
        P(("section", "chain"), "tp"),
        P(("section", "chain"), "tp"),
        P("tp", ("section", "chain")),
        P("section", "chain", None, None, "tp"),
        P("chain", None),
        P("chain"),
        P("chain", "section", None),
    )
    out_specs = (P("section", "chain", None, "tp"), P("section", "chain", None, None, "tp"))
    return jax.shard_map(local, mesh=mesh, in_specs=in_specs, out_specs=out_specs, check_vma=False)
```

time: 1420 us -> 236 us (0.17)
  waiting for transfers between devices: 1200 us -> 0 us
  Pallas kernels: 0 us -> 229 us
  matrix products: 126 us -> 0 us
  other arithmetic: 35.5 us -> 1.61 us
  local copies, waits for them, and re-layouts: 28 us -> 3.55 us
    all_gather x4 -> x0, waiting for transfers between devices: 910 us -> none  [the longest x1 363 us: local(): lax.all_gather(w_query, ('section', 'chain'), axis=0, tiled=True)]
    pallas_call x0 -> x1, Pallas kernels: none -> 229 us  [local(): pl.pallas_call(kernel, out_shape=(jax.ShapeDtypeStruct((NEW, WIDTH // NTP...]
    psum x5 -> x0, waiting for transfers between devices: 213 us -> none  [advance(): lax.psum(partial_sum.astype(jnp.bfloat16), 'tp').astype(jnp.float32)]
    dot_general x26 -> x0, matrix products: 126 us -> none  [the longest x5 47.8 us: advance(): jnp.dot(mixed_rows, output_full, preferred_element_type=jnp.float32)]
    ppermute x5 -> x0, waiting for transfers between devices: 69.6 us -> none  [shifted(): return lax.ppermute(block, axis, route)]
  transfers between devices with their start and end apart: 15 -> 0, of which waited for: 14 -> 0; matrix products, arithmetic and copies ran while one was open for 2% -> 0% of each run, Pallas kernels for 0% -> 0%
where the time goes in v1:
time: 236 us
  Pallas kernels  229 us (97%)
  local copies, waits for them, and re-layouts  3.55 us (2%)
    pallas_call x1, Pallas kernels, local(): pl.pallas_call(kernel, out_shape=(jax.ShapeDtypeStruct((NEW, WIDTH // NTP...  229 us

profile of v1, /device:TPU:25, one launch (start us, length us, event | category | flops | bytes accessed | tf_op | source)
XLA Modules:
  0.0 235.5 jit_solution(10431384029275229123)
XLA Ops:
  0.6 0.8 dynamic-slice_convert_fusion
  1.4 1.3 copy.15
  2.7 0.1 multiply_convert_fusion
  2.8 0.2 copy.17
  3.0 0.0 copy-done.2
  3.0 0.1 copy.16
  3.2 0.0 copy-start.3
  3.2 0.0 copy-start.4
  3.2 0.0 copy-start
  3.2 0.0 copy-start.1
  3.2 0.1 multiply_convert_fusion.1
  3.3 0.2 copy.18
  3.4 0.1 maximum_bitcast_fusion.wsend
  4.2 0.2 fusion.1
  4.4 0.1 pad_maximum_fusion
  4.5 0.1 select_reduce_fusion
  4.6 0.1 mul.67
  4.7 0.1 add.45
  4.8 0.1 add.46
  4.9 0.1 add.48
  5.0 0.2 convert_reduce_fusion
  5.3 228.9 %shard_map.104 = (bf16[64,2048]{1,0:T(8,128)(2,1)S(1)}, bf16[4,32,512]{2,1,0:T(8,128)(2,1)S(1)}) custom-call(bf16[64,2048]{1,0:T(8,128)(2,1)S(1)} %bitcast.14, bf16[4,256,384]{2,1,0:T(8,128)(2,1)S(1)} %maximum_bitcast_fusion.wsend, bf16[1024,256]{1,0:T(8,128)(2,1)S(1)} %copy-done, bf16[4096,512]{1,0:T(8,128)(2,1)} %bitcast.17, f32[8,512]{1,0:T(8,128)S(1)} %fusion.bias, ...), custom_call_target="tpu_custom_call" | custom-call | tf_op jit(solution)/shard_map/pallas_call | solution.py:524
  234.2 0.7 copy.22
  234.9 0.7 copy.23
  (12 shorter events, 0.1 us)
Async XLA Ops:
  1.4 1.6 copy-start.2
  3.2 1.3 copy-start.3
  3.2 1.9 copy-start.4
  3.2 2.1 copy-start
  3.2 2.1 copy-start.1

commit v2 on v1

v2 whole, which is shorter than its diff:
```python
import math

import jax
import jax.numpy as jnp
from jax import lax
from jax.experimental import pallas as pl
from jax.experimental.pallas import tpu as pltpu
from jax.sharding import PartitionSpec as P

HD = 128
PAGE = 16
PREFIX = 4096
NEW = 64
WIDTH = 8192
NSEC = 4
NCH = 8
NTP = 4
QC = 256
PC = 384
CH = 512
NCHUNK = PREFIX // CH
STREAMS = ((0, 32), (32, 32))
NS = len(STREAMS)
SKEW = 0
R = STREAMS[0][1]
MESH = pl.DeviceIdType.MESH
BF = jnp.bfloat16
F32 = jnp.float32


def kernel(
    hin, wq, wkv, wo, gain, cache, bias, table, sel,
    bout, pool,
    cachev, wq_l, wo_l, hA, part1, rbuf, ssend, srecv, sbuf2, qbuf, kvnew, S, msend, mixb, osend, ob, placed, obuf, pbuf,
    csem, h0s, h0r, h2s, h2r, wqs, wqr, wks, wkr, wos, wor,
    s1, r1, ss_s, ss_r, s2, r2, s3, r3, s4, r4, s5, r5, s6, r6, s7, r7, s7f, r7f, so, ro, ps, pr,
):
    y = lax.axis_index("section")
    c = lax.axis_index("chain")
    t = lax.axis_index("tp")
    u = t // 2
    k = t % 2
    own = 2 * y + u
    twin = (y, c, 2 * u + 1 - k)

    def remote(src, dst, ssem, rsem, dev):
        return pltpu.make_async_remote_copy(
            src_ref=src, dst_ref=dst, send_sem=ssem, recv_sem=rsem, device_id=dev, device_id_type=MESH
        )

    def got(dst, rsem):
        pltpu.make_async_copy(dst, dst, rsem).wait()

    barrier = pltpu.get_barrier_semaphore()
    for d in range(1, NCH):
        pl.semaphore_signal(barrier, inc=1, device_id=(y, (c + d) % NCH, t), device_id_type=MESH)
    for dy in range(NSEC):
        for dt in range(NTP):
            if dy or dt:
                pl.semaphore_signal(
                    barrier, inc=1, device_id=((y + dy) % NSEC, c, (t + dt) % NTP), device_id_type=MESH
                )
    for g in range(NCH):
        mine = (y == c // 2) & (c == g) & (t == 2 * (c % 2) + t // 2)

        @pl.when(jnp.logical_not(mine))
        def _():
            pl.semaphore_signal(
                barrier, inc=1, device_id=(c // 2, g, 2 * (c % 2) + t // 2), device_id_type=MESH
            )

    own_dest = (c == own) & (k == u)
    pl.semaphore_wait(barrier, NCH - 1 + NSEC * NTP - 1 + 8 - own_dest.astype(jnp.int32))

    def wq_copy(d):
        peer = (y + d) % NSEC
        src = wq.at[:, pl.ds(pl.multiple_of(peer * QC, QC), QC)]
        dst = wq_l.at[y, :, pl.ds(0, QC)]
        return lambda: remote(src, dst, wqs.at[d], wqr.at[y], (peer, c, t)), src, dst

    def wkv_copy(d):
        peer = (y + d) % NSEC
        src = wkv.at[:, pl.ds(pl.multiple_of(peer * HD, HD), HD)]
        dst = wq_l.at[y, :, pl.ds(QC, HD)]
        return lambda: remote(src, dst, wks.at[d], wkr.at[y], (peer, c, t)), src, dst

    def wo_copy(d):
        peer = (y + d) % NSEC
        src = wo.at[pl.ds(pl.multiple_of(peer * QC, QC), QC), :]
        return lambda: remote(src, wo_l.at[k, y % 2], wos.at[d], wor.at[k, y % 2], (peer, c, 2 * u + y // 2)), src

    def first_hop(st, d):
        r0 = STREAMS[st][0]
        peer = (c + d) % NCH
        src = hin.at[pl.ds(r0, R), pl.ds(pl.multiple_of(peer * QC, QC), QC)]
        dst = hA.at[st, t // 2, c, :, pl.ds(pl.multiple_of((t % 2) * QC, QC), QC)]
        return lambda: remote(src, dst, h0s.at[st, d], h0r.at[st, c], (y, peer, t)), src, dst

    def columns(st, tt):
        return hA.at[st, tt // 2, :, :, pl.ds(pl.multiple_of((tt % 2) * QC, QC), QC)]

    across = 2 * (1 - u) + k
    across_twin = 2 * (1 - u) + 1 - k

    def second_hop(st, which):
        if which == 0:
            return remote(columns(st, t), columns(st, t), h2s.at[st, 0], h2r.at[st, 0], (y, c, across))
        if which == 1:
            return remote(columns(st, t), columns(st, t), h2s.at[st, 1], h2r.at[st, 1], twin)
        return remote(columns(st, across), columns(st, across), h2s.at[st, 2], h2r.at[st, 2], twin)

    for st in range(NS):
        for d in range(1, NCH):
            first_hop(st, d)[0]().start()
        _, src, dst = first_hop(st, 0)
        pltpu.make_async_copy(src, dst, h0r.at[st, c]).start()
    for d in range(1, NSEC):
        wq_copy(d)[0]().start()
        wkv_copy(d)[0]().start()
    _, src, dst = wq_copy(0)
    pltpu.make_async_copy(src, dst, wqr.at[y]).start()
    _, src, dst = wkv_copy(0)
    pltpu.make_async_copy(src, dst, wkr.at[y]).start()
    cache_copy = pltpu.make_async_copy(cache, cachev, csem)
    cache_copy.start()

    for st in range(NS):
        for d in range(NCH):
            g = (c + NCH - d) % NCH
            got(hA.at[st, t // 2, g, :, pl.ds(pl.multiple_of((t % 2) * QC, QC), QC)], h0r.at[st, g])
        second_hop(st, 0).start()
        second_hop(st, 1).start()

    for d in range(NSEC):
        g = (y + NSEC - d) % NSEC
        got(wq_l.at[g, :, pl.ds(0, QC)], wqr.at[g])
        got(wq_l.at[g, :, pl.ds(QC, HD)], wkr.at[g])
    for d in range(NSEC):
        if d:
            wo_copy(d)[0]().start()
        else:
            @pl.when(k == y // 2)
            def _():
                pltpu.make_async_copy(wo_copy(0)[1], wo_l.at[k, y % 2], wor.at[k, y % 2]).start()

            @pl.when(k != y // 2)
            def _():
                wo_copy(0)[0]().start()
    for d in range(1, NSEC):
        wq_copy(d)[0]().wait_send()
        wkv_copy(d)[0]().wait_send()
    for g in range(NSEC):
        row = gain[pl.ds(g * NCH + c, 1), :]
        column = jnp.transpose(jnp.broadcast_to(row, (128, QC)))
        for a in range(PC // 128):
            part = wq_l[g, :, a * 128:(a + 1) * 128].astype(F32) * column
            wq_l[g, :, a * 128:(a + 1) * 128] = part.astype(BF)
    for st in range(NS):
        got(columns(st, across), h2r.at[st, 0])
        second_hop(st, 2).start()
    for st in range(NS):
        got(columns(st, 2 * u + 1 - k), h2r.at[st, 1])
        got(columns(st, across_twin), h2r.at[st, 2])
        for d in range(1, NCH):
            first_hop(st, d)[0]().wait_send()
        for which in range(3):
            second_hop(st, which).wait_send()
    cache_copy.wait()

    def ag_copy(st, e):
        g = (own + e) % 8
        piece = hA.at[st, k, own]
        return remote(piece, piece, s7.at[st, e], r7.at[st, own], (g // 2, c, 2 * (g % 2) + k))

    def twin_copy(st, e):
        g = (own + 8 - e) % 8
        piece = hA.at[st, k, g]
        return remote(piece, piece, s7f.at[st, e], r7f.at[st, g], twin)

    def ag_send(st):
        for e in range(1, 8):
            ag_copy(st, e).start()
        twin_copy(st, 0).start()

    def ag_forward(st, s):
        @pl.when(s < NSEC - 1)
        def _():
            for e in range(1, 8):
                g = (own + 8 - e) % 8
                got(hA.at[st, k, g], r7.at[st, g])
                twin_copy(st, e).start()

    def ag_wait(st, s):
        @pl.when(s < NSEC - 1)
        def _():
            for e in range(8):
                g = (own + 8 - e) % 8
                got(hA.at[st, 1 - k, g], r7f.at[st, g])

    def ag_sent(st):
        for e in range(1, 8):
            ag_copy(st, e).wait_send()
        for e in range(8):
            twin_copy(st, e).wait_send()

    def p1_copy(st, d):
        peer = (c + d) % NCH
        return remote(part1.at[st, peer], rbuf.at[st, c], s1.at[st, d], r1.at[st, c], (y, peer, t))

    def ss_copy(st, d):
        peer = (c + d) % NCH
        return remote(ssend.at[st, peer], srecv.at[st, c], ss_s.at[st, d], ss_r.at[st, c], (y, peer, t))

    def project(st):
        total = None
        for half in range(2):
            x = hA[st, half].reshape(NCH * R, 512)
            w = wq_l[pl.ds(2 * half, 2)].reshape(512, PC)
            term = jnp.dot(x, w, preferred_element_type=F32)
            total = term if total is None else total + term
        part1[st] = total.astype(BF).reshape(NCH, R, PC)
        for d in range(1, NCH):
            p1_copy(st, d).start()
        ones = jnp.ones((8, 128), BF)
        for g in range(NCH):
            acc = None
            for half in range(2):
                wide = hA[st, half, g].astype(F32)
                square = wide * wide
                for a in range(4):
                    piece = square[:, a * 128:(a + 1) * 128]
                    acc = piece if acc is None else acc + piece
            high = acc.astype(BF)
            low = (acc - high.astype(F32)).astype(BF)
            dims = (((1,), (1,)), ((), ()))
            row = lax.dot_general(ones, high, dims, preferred_element_type=F32)
            row = row + lax.dot_general(ones, low, dims, preferred_element_type=F32)
            ssend[st, g] = jnp.concatenate([row, jnp.zeros((8, 128 - R), F32)], axis=1)
        for d in range(1, NCH):
            ss_copy(st, d).start()
        rbuf[st, c] = part1[st, c]
        srecv[st, c] = ssend[st, c]

    def p2_copy(st, s):
        return remote(sbuf2.at[st], qbuf.at[st, y], s2.at[st], r2.at[st, y], (s, c, t))

    def finish_projection(st, s):
        r0 = STREAMS[st][0]
        for d in range(1, NCH):
            g = (c + NCH - d) % NCH
            got(rbuf.at[st, g], r1.at[st, g])
            got(srecv.at[st, g], ss_r.at[st, g])
        total = rbuf[st, 0].astype(F32)
        squares = srecv[st, 0]
        for g in range(1, NCH):
            total = total + rbuf[st, g].astype(F32)
            squares = squares + srecv[st, g]
        inv = lax.rsqrt(squares * (1.0 / WIDTH) + 1e-05)[0:1, :R]
        eye = lax.broadcasted_iota(jnp.int32, (R, R), 0) == lax.broadcasted_iota(jnp.int32, (R, R), 1)
        scale = jnp.sum(jnp.where(eye, inv, 0.0), axis=1, keepdims=True)
        total = total * scale
        cs = table[0, r0:r0 + R, :]
        sn = table[1, r0:r0 + R, :]
        to_score = math.log2(math.e) / math.sqrt(HD)

        def rope(v):
            return v * cs + pltpu.roll(v, 64, 1) * sn

        q0 = rope(total[:, 0:128]) * to_score
        q1 = rope(total[:, 128:256]) * to_score
        kv = total[:, 256:384]
        even = (y % 2 == 0).astype(F32)
        kv = rope(kv) * even + kv * (1.0 - even)
        sbuf2[st] = jnp.concatenate([q0, q1, kv], axis=1).astype(BF)

        @pl.when(y == s)
        def _():
            qbuf[st, y] = sbuf2[st]

        @pl.when(y != s)
        def _():
            p2_copy(st, s).start()

        for d in range(1, NCH):
            p1_copy(st, d).wait_send()
            ss_copy(st, d).wait_send()

        @pl.when(s > 0)
        def _():
            ag_sent(st)
            bout_sent(st, s - 1)

    def p3_copy(st, peer):
        return remote(msend.at[st, peer], mixb.at[st, k, c], s3.at[st, peer], r3.at[st], (peer, c, t))

    def pool_copy(d):
        peer = (y + d) % NSEC
        return remote(placed.at[peer], pbuf.at[y], ps.at[d], pr.at[y], (peer, c, t))

    def attend(st):
        r0 = STREAMS[st][0]
        seen = r0 + R
        dims = (((1,), (1,)), ((), ()))
        for j in range(2):
            for g in (2 * j, 2 * j + 1):
                @pl.when(y != g)
                def _():
                    got(qbuf.at[st, g], r2.at[st, g])

                kvnew[r0:r0 + R, g * 128:(g + 1) * 128] = qbuf[st, g, :, QC:PC]
            q = jnp.concatenate(
                [qbuf[st, 2 * j + hh // 2, :, (hh % 2) * 128:(hh % 2 + 1) * 128] for hh in range(4)], axis=0
            )
            kcol = j * 256
            vcol = j * 256 + 128
            sf = lax.dot_general(q, kvnew[0:seen, kcol:kcol + 128], dims, preferred_element_type=F32)
            row = lax.broadcasted_iota(jnp.int32, (4, R, seen), 1).reshape(4 * R, seen) + r0
            col = lax.broadcasted_iota(jnp.int32, (4 * R, seen), 1)
            sf = jnp.where(col <= row, sf, -1e30)
            peak = jnp.full((4 * R, 128), -1e30, F32)
            for i in range(NCHUNK):
                keys = cachev[i * CH:(i + 1) * CH, kcol:kcol + 128]
                sc = lax.dot_general(q, keys, dims, preferred_element_type=F32) + bias[i:i + 1, :]
                S[i] = sc
                for a in range(CH // 128):
                    peak = jnp.maximum(peak, sc[:, a * 128:(a + 1) * 128])
            top = jnp.maximum(jnp.max(peak, axis=1, keepdims=True), jnp.max(sf, axis=1, keepdims=True))
            pf = jnp.exp2(sf - top)
            acc = jnp.dot(pf.astype(BF), kvnew[0:seen, vcol:vcol + 128], preferred_element_type=F32)
            den = jnp.zeros((4 * R, 128), F32)
            for i in range(NCHUNK):
                p = jnp.exp2(S[i] - top)
                for a in range(CH // 128):
                    den = den + p[:, a * 128:(a + 1) * 128]
                values = cachev[i * CH:(i + 1) * CH, vcol:vcol + 128]
                acc = acc + jnp.dot(p.astype(BF), values, preferred_element_type=F32)
            den = jnp.sum(den, axis=1, keepdims=True) + jnp.sum(pf, axis=1, keepdims=True)
            mixed = (acc / den).astype(BF)
            for hh in range(4):
                msend[st, 2 * j + hh // 2, :, (hh % 2) * 128:(hh % 2 + 1) * 128] = mixed[hh * R:(hh + 1) * R]
            for g in (2 * j, 2 * j + 1):
                @pl.when(y != g)
                def _():
                    p3_copy(st, g).start()

                @pl.when(y == g)
                def _():
                    mixb[st, k, c] = msend[st, g]

    def place_pages():
        for slot in range(2 * NSEC):
            acc = None
            for q in range(NEW // PAGE):
                term = kvnew[q * PAGE:(q + 1) * PAGE, :].astype(F32) * sel[slot, q]
                acc = term if acc is None else acc + term
            placed[slot // 2, (slot % 2) * PAGE:(slot % 2 + 1) * PAGE, :] = acc.astype(BF)
        for d in range(1, NSEC):
            pool_copy(d).start()
        pbuf[y] = placed[y]

    def mix(st, s):
        @pl.when(y == s)
        def _():
            attend(st)

        @pl.when(y != s)
        def _():
            p2_copy(st, s).wait_send()

    def p4_copy(st, d):
        peer = (c + d) % NCH
        piece = mixb.at[st, k, c]
        return remote(piece, piece, s4.at[st, d], r4.at[st, c], (y, peer, t))

    def p5_copy(st, d):
        g = (c + NCH - d) % NCH
        piece = mixb.at[st, k, g]
        return remote(piece, piece, s5.at[st, d], r5.at[st, g], twin)

    def spread(st, s):
        @pl.when(y != s)
        def _():
            got(mixb.at[st, k, c], r3.at[st])

        for d in range(1, NCH):
            p4_copy(st, d).start()
        p5_copy(st, 0).start()
        if st == NS - 1:
            @pl.when(y == s)
            def _():
                place_pages()

    def spread_twin(st):
        for d in range(1, NCH):
            g = (c + NCH - d) % NCH
            got(mixb.at[st, k, g], r4.at[st, g])
            p5_copy(st, d).start()

    def p6_copy(st, e):
        g = (own + e) % 8
        return remote(osend.at[st, g], ob.at[st, own], s6.at[st, e], r6.at[st, own], (g // 2, c, 2 * (g % 2) + k))

    def bout_copy(st, s, a):
        src = hA.at[st, k, own, :, pl.ds(a * QC, QC)]
        dst = obuf.at[c, pl.ds(STREAMS[st][0], R), :]
        return lambda: remote(src, dst, so.at[st, a], ro.at[st, c], (s, own, 2 * k + a)), src, dst

    def bout_mine(s, a):
        return (y == s) & (c == own) & (t == 2 * k + a)

    def bout_send(st, s):
        for a in range(2):
            @pl.when(bout_mine(s, a))
            def _():
                _, src, dst = bout_copy(st, s, a)
                pltpu.make_async_copy(src, dst, so.at[st, a]).start()

            @pl.when(jnp.logical_not(bout_mine(s, a)))
            def _():
                bout_copy(st, s, a)[0]().start()

    def bout_sent(st, s):
        for a in range(2):
            @pl.when(bout_mine(s, a))
            def _():
                got(bout_copy(st, s, a)[2], so.at[st, a])

            @pl.when(jnp.logical_not(bout_mine(s, a)))
            def _():
                bout_copy(st, s, a)[0]().wait_send()

    def wo_wait():
        for a in range(2):
            for b in range(2):
                got(wo_l.at[a, b], wor.at[a, b])
        for d in range(NSEC):
            if d:
                wo_copy(d)[0]().wait_send()
            else:
                @pl.when(k != y // 2)
                def _():
                    wo_copy(0)[0]().wait_send()

    def output_projection(st, s):
        for d in range(NCH):
            g = (c + NCH - d) % NCH
            got(mixb.at[st, 1 - k, g], r5.at[st, g])
        if st == 0:
            @pl.when(s == 0)
            def _():
                wo_wait()

        for b in range(2):
            total = None
            for a in range(2):
                x = mixb[st, a].reshape(NCH * R, QC)
                term = jnp.dot(x, wo_l[a, b], preferred_element_type=F32)
                total = term if total is None else total + term
            osend[st, :, :, b * QC:(b + 1) * QC] = total.astype(BF).reshape(NCH, R, QC)

        for d in range(1, NCH):
            p4_copy(st, d).wait_send()
        for d in range(NCH):
            p5_copy(st, d).wait_send()

        @pl.when(y == s)
        def _():
            for g in range(NSEC):
                @pl.when(y != g)
                def _():
                    p3_copy(st, g).wait_send()

        for e in range(1, 8):
            p6_copy(st, e).start()
        ob[st, own] = osend[st, own]

    def residual(st, s):
        for e in range(1, 8):
            g = (own + 8 - e) % 8
            got(ob.at[st, g], r6.at[st, g])
        total = ob[st, 0].astype(F32)
        for g in range(1, 8):
            total = total + ob[st, g].astype(F32)
        hA[st, k, own] = (hA[st, k, own].astype(F32) + total).astype(BF)

        @pl.when(s < NSEC - 1)
        def _():
            ag_send(st)

        bout_send(st, s)
        for e in range(1, 8):
            p6_copy(st, e).wait_send()

    phases = [
        lambda st, s: project(st),
        finish_projection,
        mix,
        spread,
        lambda st, s: spread_twin(st),
        output_projection,
        residual,
        ag_forward,
        ag_wait,
    ]
    n = len(phases)

    def section_step(s, carry):
        for i in range(n):
            phases[i](0, s)
            for st in range(1, NS):
                if i >= SKEW:
                    phases[i - SKEW](st, s)
                else:
                    @pl.when(s > 0)
                    def _():
                        phases[n + i - SKEW](st, s - 1)
        return carry

    lax.fori_loop(0, NSEC, section_step, 0)
    for i in range(SKEW):
        for st in range(1, NS):
            phases[n + i - SKEW](st, NSEC - 1)

    for st in range(NS):
        bout_sent(st, NSEC - 1)
        for d in range(NCH):
            g = (c + d) % NCH
            mine = (y == c // 2) & (c == g) & (t == 2 * (c % 2) + t // 2)

            @pl.when(jnp.logical_not(mine))
            def _():
                got(obuf.at[g, pl.ds(STREAMS[st][0], R), :], ro.at[st, g])
    for d in range(1, NSEC):
        g = (y + NSEC - d) % NSEC
        got(pbuf.at[g], pr.at[g])
        pool_copy(d).wait_send()
    for g in range(NCH):
        bout[:, g * QC:(g + 1) * QC] = obuf[g]
    for g in range(NSEC):
        pool[g] = pbuf[g]


def local(block_input, norm_gain, w_query, w_kv, w_out, kv_cache, page_table, prefix_len, page_owner):
    length = prefix_len[0]
    gain = norm_gain.astype(F32).reshape(NSEC * NCH, WIDTH // (NSEC * NCH))

    pages = PREFIX // PAGE
    ids = jnp.arange(pages, dtype=jnp.int32)
    logical = jnp.sum(jnp.where(page_table[0][None, :] == ids[:, None], ids[None, :], 0), axis=1)
    place = logical[:, None] * PAGE + jnp.arange(PAGE, dtype=jnp.int32)[None, :]
    bias = jnp.where(place < length, 0.0, -1e30).astype(F32).reshape(NCHUNK, CH)

    lane = jnp.arange(HD)
    inverse = 500000.0 ** (-((lane % (HD // 2)).astype(F32) * 2.0 / HD))
    angles = (length + jnp.arange(NEW)).astype(F32)[:, None] * inverse[None, :]
    sine = jnp.where(lane[None, :] < HD // 2, -1.0, 1.0) * jnp.sin(angles)
    table = jnp.stack([jnp.cos(angles), sine])

    owners = page_owner[0, :, 0]
    q = jnp.arange(NEW // PAGE)
    earlier = (owners[:, None] == owners[None, :]) & (q[None, :] < q[:, None])
    slots = owners * 2 + jnp.sum(earlier.astype(jnp.int32), axis=1)
    sel = (slots[None, :] == jnp.arange(2 * NSEC)[:, None]).astype(F32)

    vm = pl.BlockSpec(memory_space=pltpu.VMEM)
    hbm = pl.BlockSpec(memory_space=pl.ANY)
    dma = pltpu.SemaphoreType.DMA
    V = pltpu.VMEM
    bout, pool = pl.pallas_call(
        kernel,
        out_shape=(
            jax.ShapeDtypeStruct((NEW, WIDTH // NTP), BF),
            jax.ShapeDtypeStruct((NSEC, 2 * PAGE, 512), BF),
        ),
        in_specs=[vm, hbm, hbm, hbm, vm, hbm, vm, vm, pl.BlockSpec(memory_space=pltpu.SMEM)],
        out_specs=(vm, vm),
        scratch_shapes=[
            V((PREFIX, 512), BF),
            V((NSEC, 256, PC), BF),
            V((2, 2, 256, 256), BF),
            V((NS, 2, NCH, R, 512), BF),
            V((NS, NCH, R, PC), BF),
            V((NS, NCH, R, PC), BF),
            V((NS, NCH, 8, 128), F32),
            V((NS, NCH, 8, 128), F32),
            V((NS, R, PC), BF),
            V((NS, NSEC, R, PC), BF),
            V((NEW, 512), BF),
            V((NCHUNK, 4 * R, CH), F32),
            V((NS, NSEC, R, QC), BF),
            V((NS, 2, NCH, R, QC), BF),
            V((NS, NCH, R, 512), BF),
            V((NS, NCH, R, 512), BF),
            V((NSEC, 2 * PAGE, 512), BF),
            V((NCH, NEW, QC), BF),
            V((NSEC, 2 * PAGE, 512), BF),
            dma(()),
            dma((NS, NCH)), dma((NS, NCH)),
            dma((NS, 3)), dma((NS, 3)),
            dma((NSEC,)), dma((NSEC,)),
            dma((NSEC,)), dma((NSEC,)),
            dma((NSEC,)), dma((2, 2)),
            dma((NS, NCH)), dma((NS, NCH)),
            dma((NS, NCH)), dma((NS, NCH)),
            dma((NS,)), dma((NS, NSEC)),
            dma((NS, NSEC)), dma((NS,)),
            dma((NS, NCH)), dma((NS, NCH)),
            dma((NS, NCH)), dma((NS, NCH)),
            dma((NS, 8)), dma((NS, 8)),
            dma((NS, 8)), dma((NS, 8)),
            dma((NS, 8)), dma((NS, 8)),
            dma((NS, 2)), dma((NS, NCH)),
            dma((NSEC,)), dma((NSEC,)),
        ],
        compiler_params=pltpu.CompilerParams(
            collective_id=0, has_side_effects=True, vmem_limit_bytes=48 * 1024 * 1024
        ),
    )(block_input[0], w_query, w_kv, w_out, gain, kv_cache.reshape(PREFIX, 512), bias, table, sel)
    return bout[None, None], pool.reshape(1, 1, 2 * NSEC, PAGE, 512)


def solution(mesh):
    in_specs = (
        P("chain", None, "tp"),
        P(),
        P(("section", "chain"), "tp"),
        P(("section", "chain"), "tp"),
        P("tp", ("section", "chain")),
        P("section", "chain", None, None, "tp"),
        P("chain", None),
        P("chain"),
        P("chain", "section", None),
    )
    out_specs = (P("section", "chain", None, "tp"), P("section", "chain", None, None, "tp"))
    return jax.shard_map(local, mesh=mesh, in_specs=in_specs, out_specs=out_specs, check_vma=False)
```

time: 236 us -> 185 us (0.78)
  Pallas kernels: 229 us -> 175 us
  local copies, waits for them, and re-layouts: 3.55 us -> 6.43 us
    pallas_call x1, Pallas kernels: 229 us -> 175 us  [local(): pl.pallas_call(kernel, out_shape=(jax.ShapeDtypeStruct((NEW, WIDTH // NTP...]
    unnamed x14 -> x10, local copies, waits for them, and re-layouts: 2.81 us -> 5.34 us
where the time goes in v2:
time: 185 us
  Pallas kernels  175 us (95%)
  local copies, waits for them, and re-layouts  6.43 us (3%)
  other arithmetic  2.59 us (1%)
    pallas_call x1, Pallas kernels, local(): pl.pallas_call(kernel, out_shape=(jax.ShapeDtypeStruct((NEW, WIDTH // NTP...  175 us
    unnamed x10, local copies, waits for them, and re-layouts  5.34 us

profile of v2, /device:TPU:25, one launch (start us, length us, event | category | flops | bytes accessed | tf_op | source)
XLA Modules:
  0.0 185.0 jit_solution(12350623829636114022)
XLA Ops:
  1.3 0.9 convert_reduce_fusion
  2.2 0.7 multiply_add_fusion
  2.9 0.8 select_reduce_fusion
  3.7 0.1 mul.65
  3.8 0.1 add.50
  3.8 0.7 reshape.180.gain
  4.6 0.2 multiply_cosine_fusion
  4.8 0.1 add.47
  4.9 0.1 add.48
  5.0 0.0 copy-start
  5.0 1.0 copy-done
  6.1 0.0 copy-start.1
  6.1 1.0 copy-done.1
  7.1 0.0 copy-start.2
  7.1 0.9 copy-done.2
  8.1 0.0 copy-start.3
  8.1 0.9 copy-done.3
  9.0 174.6 %shard_map.104 = (bf16[64,2048]{1,0:T(8,128)(2,1)S(1)}, bf16[4,32,512]{2,1,0:T(8,128)(2,1)S(1)}) custom-call(bf16[64,2048]{1,0:T(8,128)(2,1)S(1)} %bitcast.10, bf16[256,1024]{1,0:T(8,128)(2,1)S(1)} %copy-done, bf16[256,512]{1,0:T(8,128)(2,1)S(1)} %copy-done.3, bf16[1024,256]{1,0:T(8,128)(2,1)S(1)} %copy-done.1, f32[32,256]{1,0:T(8,128)S(1)} %reshape.180.gain, ...), custom_call_target="tpu_custom_call" | custom-call | tf_op jit(solution)/shard_map/pallas_call | solution.py:569
  183.6 0.7 copy.14
  184.3 0.7 copy.15
  (7 shorter events, 0.0 us)
Async XLA Ops:
  5.0 1.0 copy-start
  6.1 1.0 copy-start.1
  7.1 0.9 copy-start.2
  8.1 0.9 copy-start.3

commit v3 on v2

--- a/solution.py
+++ b/solution.py
@@ -21,7 +21,6 @@
 NCHUNK = PREFIX // CH
 STREAMS = ((0, 32), (32, 32))
 NS = len(STREAMS)
-SKEW = 0
 R = STREAMS[0][1]
 MESH = pl.DeviceIdType.MESH
 BF = jnp.bfloat16
@@ -29,10 +28,10 @@
 
 
 def kernel(
-    hin, wq, wkv, wo, gain, cache, bias, table, sel,
+    hin, wq, wkv, wo, gain_in, cache, pages_in, cos_in, sin_in, length, owner,
     bout, pool,
-    cachev, wq_l, wo_l, hA, part1, rbuf, ssend, srecv, sbuf2, qbuf, kvnew, S, msend, mixb, osend, ob, placed, obuf, pbuf,
-    csem, h0s, h0r, h2s, h2r, wqs, wqr, wks, wkr, wos, wor,
+    gain, pages, cosv, sinv, bias, cachev, wq_l, wo_l, hA, part1, rbuf, ssend, srecv, sbuf2, qbuf, kvnew, S, msend, mixb, osend, ob, placed, obuf, pbuf,
+    insem, csem, h0s, h0r, h2s, h2r, wqs, wqr, wks, wkr, wos, wor,
     s1, r1, ss_s, ss_r, s2, r2, s3, r3, s4, r4, s5, r5, s6, r6, s7, r7, s7f, r7f, so, ro, ps, pr,
 ):
     y = lax.axis_index("section")
@@ -51,9 +50,18 @@
     def got(dst, rsem):
         pltpu.make_async_copy(dst, dst, rsem).wait()
 
+    inputs = ((gain_in, gain), (pages_in, pages), (cos_in, cosv), (sin_in, sinv))
+    for i, (src, dst) in enumerate(inputs):
+        pltpu.make_async_copy(src, dst, insem.at[i]).start()
+    cache_copy = pltpu.make_async_copy(cache, cachev, csem)
+    cache_copy.start()
+    across = 2 * (1 - u) + k
+    across_twin = 2 * (1 - u) + 1 - k
+
     barrier = pltpu.get_barrier_semaphore()
     for d in range(1, NCH):
         pl.semaphore_signal(barrier, inc=1, device_id=(y, (c + d) % NCH, t), device_id_type=MESH)
+        pl.semaphore_signal(barrier, inc=1, device_id=(y, (c + d) % NCH, across), device_id_type=MESH)
     for dy in range(NSEC):
         for dt in range(NTP):
             if dy or dt:
@@ -70,7 +78,28 @@
             )
 
     own_dest = (c == own) & (k == u)
-    pl.semaphore_wait(barrier, NCH - 1 + NSEC * NTP - 1 + 8 - own_dest.astype(jnp.int32))
+
+    for i, (src, dst) in enumerate(inputs):
+        pltpu.make_async_copy(src, dst, insem.at[i]).wait()
+    n_pages = PREFIX // PAGE
+    logical = lax.broadcasted_iota(jnp.int32, (8, n_pages), 1)
+    live = jnp.clip(length[0] - logical * PAGE, 0, PAGE).astype(F32).astype(BF)
+    physical = lax.broadcasted_iota(jnp.int32, (n_pages, n_pages), 0)
+    named = jnp.where(pages[...] == physical, 1.0, 0.0).astype(BF)
+    rows_live = lax.dot_general(live, named, (((1,), (1,)), ((), ())), preferred_element_type=F32)
+    chunk_pages = CH // PAGE
+    first = lax.broadcasted_iota(jnp.int32, (NCHUNK, n_pages), 0) * chunk_pages
+    page = lax.broadcasted_iota(jnp.int32, (NCHUNK, n_pages), 1)
+    held = jnp.where((page >= first) & (page < first + chunk_pages), rows_live, 0.0).astype(BF)
+    key = lax.broadcasted_iota(jnp.int32, (n_pages, CH), 1)
+    page_in = lax.rem(lax.broadcasted_iota(jnp.int32, (n_pages, CH), 0), chunk_pages)
+    start = page_in * PAGE
+    spread_to = jnp.where((key >= start) & (key < start + PAGE), 1.0, 0.0).astype(BF)
+    count = jnp.dot(held, spread_to, preferred_element_type=F32)
+    row_in = lax.rem(lax.broadcasted_iota(jnp.int32, (NCHUNK, CH), 1), PAGE).astype(F32)
+    bias[...] = jnp.where(row_in + 0.5 < count, 0.0, -1e30)
+
+    pl.semaphore_wait(barrier, 2 * (NCH - 1) + NSEC * NTP - 1 + 8 - own_dest.astype(jnp.int32))
 
     def wq_copy(d):
         peer = (y + d) % NSEC
@@ -89,31 +118,37 @@
         src = wo.at[pl.ds(pl.multiple_of(peer * QC, QC), QC), :]
         return lambda: remote(src, wo_l.at[k, y % 2], wos.at[d], wor.at[k, y % 2], (peer, c, 2 * u + y // 2)), src
 
-    def first_hop(st, d):
-        r0 = STREAMS[st][0]
+    def first_hop(st, d, far):
         peer = (c + d) % NCH
-        src = hin.at[pl.ds(r0, R), pl.ds(pl.multiple_of(peer * QC, QC), QC)]
+        src = hin.at[pl.ds(STREAMS[st][0], R), pl.ds(pl.multiple_of(peer * QC, QC), QC)]
         dst = hA.at[st, t // 2, c, :, pl.ds(pl.multiple_of((t % 2) * QC, QC), QC)]
-        return lambda: remote(src, dst, h0s.at[st, d], h0r.at[st, c], (y, peer, t)), src, dst
+        dev = (y, peer, across if far else t)
+        return lambda: remote(src, dst, h0s.at[st, far, d], h0r.at[st, far, c], dev), src, dst
 
     def columns(st, tt):
         return hA.at[st, tt // 2, :, :, pl.ds(pl.multiple_of((tt % 2) * QC, QC), QC)]
 
-    across = 2 * (1 - u) + k
-    across_twin = 2 * (1 - u) + 1 - k
-
-    def second_hop(st, which):
-        if which == 0:
-            return remote(columns(st, t), columns(st, t), h2s.at[st, 0], h2r.at[st, 0], (y, c, across))
-        if which == 1:
-            return remote(columns(st, t), columns(st, t), h2s.at[st, 1], h2r.at[st, 1], twin)
-        return remote(columns(st, across), columns(st, across), h2s.at[st, 2], h2r.at[st, 2], twin)
-
-    for st in range(NS):
-        for d in range(1, NCH):
-            first_hop(st, d)[0]().start()
-        _, src, dst = first_hop(st, 0)
-        pltpu.make_async_copy(src, dst, h0r.at[st, c]).start()
+    def second_hop(st, far):
+        piece = columns(st, across if far else t)
+        return remote(piece, piece, h2s.at[st, far], h2r.at[st, far], twin)
+
+    def first_sends(st):
+        _, src, dst = first_hop(st, 0, 0)
+        pltpu.make_async_copy(src, dst, h0r.at[st, 0, c]).start()
+        first_hop(st, 0, 1)[0]().start()
+        for d in range(1, NCH):
+            first_hop(st, d, 0)[0]().start()
+            first_hop(st, d, 1)[0]().start()
+
+    def second_sends(st):
+        for far in range(2):
+            tt = across if far else t
+            for d in range(NCH):
+                g = (c + NCH - d) % NCH
+                got(hA.at[st, tt // 2, g, :, pl.ds(pl.multiple_of((tt % 2) * QC, QC), QC)], h0r.at[st, far, g])
+            second_hop(st, far).start()
+
+    first_sends(0)
     for d in range(1, NSEC):
         wq_copy(d)[0]().start()
         wkv_copy(d)[0]().start()
@@ -121,20 +156,8 @@
     pltpu.make_async_copy(src, dst, wqr.at[y]).start()
     _, src, dst = wkv_copy(0)
     pltpu.make_async_copy(src, dst, wkr.at[y]).start()
-    cache_copy = pltpu.make_async_copy(cache, cachev, csem)
-    cache_copy.start()
-
-    for st in range(NS):
-        for d in range(NCH):
-            g = (c + NCH - d) % NCH
-            got(hA.at[st, t // 2, g, :, pl.ds(pl.multiple_of((t % 2) * QC, QC), QC)], h0r.at[st, g])
-        second_hop(st, 0).start()
-        second_hop(st, 1).start()
-
-    for d in range(NSEC):
-        g = (y + NSEC - d) % NSEC
-        got(wq_l.at[g, :, pl.ds(0, QC)], wqr.at[g])
-        got(wq_l.at[g, :, pl.ds(QC, HD)], wkr.at[g])
+    for st in range(1, NS):
+        first_sends(st)
     for d in range(NSEC):
         if d:
             wo_copy(d)[0]().start()
@@ -146,26 +169,36 @@
             @pl.when(k != y // 2)
             def _():
                 wo_copy(0)[0]().start()
-    for d in range(1, NSEC):
-        wq_copy(d)[0]().wait_send()
-        wkv_copy(d)[0]().wait_send()
-    for g in range(NSEC):
+
+    second_sends(0)
+    for d in range(NSEC):
+        g = (y + NSEC - d) % NSEC
+        got(wq_l.at[g, :, pl.ds(0, QC)], wqr.at[g])
+        got(wq_l.at[g, :, pl.ds(QC, HD)], wkr.at[g])
         row = gain[pl.ds(g * NCH + c, 1), :]
         column = jnp.transpose(jnp.broadcast_to(row, (128, QC)))
         for a in range(PC // 128):
             part = wq_l[g, :, a * 128:(a + 1) * 128].astype(F32) * column
             wq_l[g, :, a * 128:(a + 1) * 128] = part.astype(BF)
-    for st in range(NS):
-        got(columns(st, across), h2r.at[st, 0])
-        second_hop(st, 2).start()
-    for st in range(NS):
-        got(columns(st, 2 * u + 1 - k), h2r.at[st, 1])
-        got(columns(st, across_twin), h2r.at[st, 2])
-        for d in range(1, NCH):
-            first_hop(st, d)[0]().wait_send()
-        for which in range(3):
-            second_hop(st, which).wait_send()
-    cache_copy.wait()
+    for st in range(1, NS):
+        second_sends(st)
+
+    def first_wait(st):
+        got(columns(st, 2 * u + 1 - k), h2r.at[st, 0])
+        got(columns(st, across_twin), h2r.at[st, 1])
+
+    def prologue_sent():
+        for d in range(1, NSEC):
+            wq_copy(d)[0]().wait_send()
+            wkv_copy(d)[0]().wait_send()
+        for st in range(NS):
+            first_hop(st, 0, 1)[0]().wait_send()
+            for d in range(1, NCH):
+                first_hop(st, d, 0)[0]().wait_send()
+                first_hop(st, d, 1)[0]().wait_send()
+            for far in range(2):
+                second_hop(st, far).wait_send()
+        cache_copy.wait()
 
     def ag_copy(st, e):
         g = (own + e) % 8
@@ -191,7 +224,11 @@
                 twin_copy(st, e).start()
 
     def ag_wait(st, s):
-        @pl.when(s < NSEC - 1)
+        @pl.when(s == 0)
+        def _():
+            first_wait(st)
+
+        @pl.when(s > 0)
         def _():
             for e in range(8):
                 g = (own + 8 - e) % 8
@@ -211,7 +248,8 @@
         peer = (c + d) % NCH
         return remote(ssend.at[st, peer], srecv.at[st, c], ss_s.at[st, d], ss_r.at[st, c], (y, peer, t))
 
-    def project(st):
+    def project(st, s):
+        ag_wait(st, s)
         total = None
         for half in range(2):
             x = hA[st, half].reshape(NCH * R, 512)
@@ -259,8 +297,8 @@
         eye = lax.broadcasted_iota(jnp.int32, (R, R), 0) == lax.broadcasted_iota(jnp.int32, (R, R), 1)
         scale = jnp.sum(jnp.where(eye, inv, 0.0), axis=1, keepdims=True)
         total = total * scale
-        cs = table[0, r0:r0 + R, :]
-        sn = table[1, r0:r0 + R, :]
+        cs = cosv[r0:r0 + R, :]
+        sn = sinv[r0:r0 + R, :]
         to_score = math.log2(math.e) / math.sqrt(HD)
 
         def rope(v):
@@ -288,7 +326,12 @@
         @pl.when(s > 0)
         def _():
             ag_sent(st)
-            bout_sent(st, s - 1)
+            bout_send(st, s - 1)
+
+        if st == 0:
+            @pl.when(s == 0)
+            def _():
+                prologue_sent()
 
     def p3_copy(st, peer):
         return remote(msend.at[st, peer], mixb.at[st, k, c], s3.at[st, peer], r3.at[st], (peer, c, t))
@@ -351,7 +394,11 @@
         for slot in range(2 * NSEC):
             acc = None
             for q in range(NEW // PAGE):
-                term = kvnew[q * PAGE:(q + 1) * PAGE, :].astype(F32) * sel[slot, q]
+                rank = jnp.int32(0)
+                for before in range(q):
+                    rank = rank + jnp.where(owner[before] == owner[q], 1, 0)
+                factor = jnp.where(owner[q] * 2 + rank == slot, 1.0, 0.0)
+                term = kvnew[q * PAGE:(q + 1) * PAGE, :].astype(F32) * factor
                 acc = term if acc is None else acc + term
             placed[slot // 2, (slot % 2) * PAGE:(slot % 2 + 1) * PAGE, :] = acc.astype(BF)
         for d in range(1, NSEC):
@@ -390,7 +437,7 @@
             def _():
                 place_pages()
 
-    def spread_twin(st):
+    def spread_twin(st, s):
         for d in range(1, NCH):
             g = (c + NCH - d) % NCH
             got(mixb.at[st, k, g], r4.at[st, g])
@@ -458,6 +505,9 @@
                 total = term if total is None else total + term
             osend[st, :, :, b * QC:(b + 1) * QC] = total.astype(BF).reshape(NCH, R, QC)
 
+        for e in range(1, 8):
+            p6_copy(st, e).start()
+        ob[st, own] = osend[st, own]
         for d in range(1, NCH):
             p4_copy(st, d).wait_send()
         for d in range(NCH):
@@ -470,9 +520,9 @@
                 def _():
                     p3_copy(st, g).wait_send()
 
-        for e in range(1, 8):
-            p6_copy(st, e).start()
-        ob[st, own] = osend[st, own]
+        @pl.when(s > 0)
+        def _():
+            bout_sent(st, s - 1)
 
     def residual(st, s):
         for e in range(1, 8):
@@ -487,39 +537,26 @@
         def _():
             ag_send(st)
 
-        bout_send(st, s)
+        @pl.when(s == NSEC - 1)
+        def _():
+            bout_send(st, s)
+
         for e in range(1, 8):
             p6_copy(st, e).wait_send()
 
-    phases = [
-        lambda st, s: project(st),
-        finish_projection,
-        mix,
-        spread,
-        lambda st, s: spread_twin(st),
-        output_projection,
-        residual,
-        ag_forward,
-        ag_wait,
-    ]
-    n = len(phases)
+    def attend_and_spread(st, s):
+        mix(st, s)
+        spread(st, s)
 
     def section_step(s, carry):
-        for i in range(n):
-            phases[i](0, s)
-            for st in range(1, NS):
-                if i >= SKEW:
-                    phases[i - SKEW](st, s)
-                else:
-                    @pl.when(s > 0)
-                    def _():
-                        phases[n + i - SKEW](st, s - 1)
+        for phase in (
+            project, finish_projection, attend_and_spread, spread_twin, output_projection, residual, ag_forward
+        ):
+            for st in range(NS):
+                phase(st, s)
         return carry
 
     lax.fori_loop(0, NSEC, section_step, 0)
-    for i in range(SKEW):
-        for st in range(1, NS):
-            phases[n + i - SKEW](st, NSEC - 1)
 
     for st in range(NS):
         bout_sent(st, NSEC - 1)
@@ -544,26 +581,12 @@
     length = prefix_len[0]
     gain = norm_gain.astype(F32).reshape(NSEC * NCH, WIDTH // (NSEC * NCH))
 
-    pages = PREFIX // PAGE
-    ids = jnp.arange(pages, dtype=jnp.int32)
-    logical = jnp.sum(jnp.where(page_table[0][None, :] == ids[:, None], ids[None, :], 0), axis=1)
-    place = logical[:, None] * PAGE + jnp.arange(PAGE, dtype=jnp.int32)[None, :]
-    bias = jnp.where(place < length, 0.0, -1e30).astype(F32).reshape(NCHUNK, CH)
-
     lane = jnp.arange(HD)
     inverse = 500000.0 ** (-((lane % (HD // 2)).astype(F32) * 2.0 / HD))
     angles = (length + jnp.arange(NEW)).astype(F32)[:, None] * inverse[None, :]
     sine = jnp.where(lane[None, :] < HD // 2, -1.0, 1.0) * jnp.sin(angles)
-    table = jnp.stack([jnp.cos(angles), sine])
-
-    owners = page_owner[0, :, 0]
-    q = jnp.arange(NEW // PAGE)
-    earlier = (owners[:, None] == owners[None, :]) & (q[None, :] < q[:, None])
-    slots = owners * 2 + jnp.sum(earlier.astype(jnp.int32), axis=1)
-    sel = (slots[None, :] == jnp.arange(2 * NSEC)[:, None]).astype(F32)
-
     vm = pl.BlockSpec(memory_space=pltpu.VMEM)
-    hbm = pl.BlockSpec(memory_space=pl.ANY)
+    hbm = pl.BlockSpec(memory_space=pltpu.HBM)
     dma = pltpu.SemaphoreType.DMA
     V = pltpu.VMEM
     bout, pool = pl.pallas_call(
@@ -572,9 +595,14 @@
             jax.ShapeDtypeStruct((NEW, WIDTH // NTP), BF),
             jax.ShapeDtypeStruct((NSEC, 2 * PAGE, 512), BF),
         ),
-        in_specs=[vm, hbm, hbm, hbm, vm, hbm, vm, vm, pl.BlockSpec(memory_space=pltpu.SMEM)],
+        in_specs=[hbm] * 9 + [pl.BlockSpec(memory_space=pltpu.SMEM)] * 2,
         out_specs=(vm, vm),
         scratch_shapes=[
+            V((NSEC * NCH, QC), F32),
+            V((1, PREFIX // PAGE), jnp.int32),
+            V((NEW, HD), F32),
+            V((NEW, HD), F32),
+            V((NCHUNK, CH), F32),
             V((PREFIX, 512), BF),
             V((NSEC, 256, PC), BF),
             V((2, 2, 256, 256), BF),
@@ -594,9 +622,9 @@
             V((NSEC, 2 * PAGE, 512), BF),
             V((NCH, NEW, QC), BF),
             V((NSEC, 2 * PAGE, 512), BF),
-            dma(()),
-            dma((NS, NCH)), dma((NS, NCH)),
-            dma((NS, 3)), dma((NS, 3)),
+            dma((4,)), dma(()),
+            dma((NS, 2, NCH)), dma((NS, 2, NCH)),
+            dma((NS, 2)), dma((NS, 2)),
             dma((NSEC,)), dma((NSEC,)),
             dma((NSEC,)), dma((NSEC,)),
             dma((NSEC,)), dma((2, 2)),
@@ -613,9 +641,12 @@
             dma((NSEC,)), dma((NSEC,)),
         ],
         compiler_params=pltpu.CompilerParams(
-            collective_id=0, has_side_effects=True, vmem_limit_bytes=48 * 1024 * 1024
+            collective_id=0, has_side_effects=True, vmem_limit_bytes=56 * 1024 * 1024
         ),
-    )(block_input[0], w_query, w_kv, w_out, gain, kv_cache.reshape(PREFIX, 512), bias, table, sel)
+    )(
+        block_input[0], w_query, w_kv, w_out, gain, kv_cache.reshape(PREFIX, 512), page_table,
+        jnp.cos(angles), sine, prefix_len, page_owner[0, :, 0],
+    )
     return bout[None, None], pool.reshape(1, 1, 2 * NSEC, PAGE, 512)
 
 

time: 185 us -> 177 us (0.957)
  Pallas kernels: 175 us -> 170 us
    pallas_call x1, Pallas kernels: 175 us -> 170 us  [local(): pl.pallas_call(kernel, out_shape=(jax.ShapeDtypeStruct((NEW, WIDTH // NTP...]
    unnamed x10 -> x2, local copies, waits for them, and re-layouts: 5.34 us -> 3.24 us
where the time goes in v3:
time: 177 us; the launch traced here: 176 us
  Pallas kernels  170 us (96%)
  local copies, waits for them, and re-layouts  4.58 us (3%)
    pallas_call x1, Pallas kernels, local(): pl.pallas_call(kernel, out_shape=(jax.ShapeDtypeStruct((NEW, WIDTH // NTP...  170 us

profile of v3, /device:TPU:25, one launch (start us, length us, event | category | flops | bytes accessed | tf_op | source)
XLA Modules:
  0.0 176.3 jit_solution(10849924246099477361)
XLA Ops:
  1.3 1.3 reshape.45.gain_in
  2.6 0.8 fusion
  3.5 169.6 %shard_map.104 = (bf16[64,2048]{1,0:T(8,128)(2,1)}, bf16[4,32,512]{2,1,0:T(8,128)(2,1)}) custom-call(bf16[64,2048]{1,0:T(8,128)(2,1)} %bitcast.9, bf16[256,1024]{1,0:T(8,128)(2,1)} %wq.1, bf16[256,512]{1,0:T(8,128)(2,1)} %wkv.1, bf16[1024,256]{1,0:T(8,128)(2,1)} %wo.1, f32[32,256]{1,0:T(8,128)} %reshape.45.gain_in, bf16[4096,512]{1,0:T(8,128)(2,1)} %bitcast.7, ...), custom_call_target="tpu_custom_call" | custom-call | tf_op jit(solution)/shard_map/pallas_call | solution.py:592
  173.0 1.7 copy.14
  174.7 1.6 copy.15
  (2 shorter events, 0.0 us)

commit v4 on v3

--- a/solution.py
+++ b/solution.py
@@ -2,6 +2,7 @@
 
 import jax
 import jax.numpy as jnp
+import numpy as np
 from jax import lax
 from jax.experimental import pallas as pl
 from jax.experimental.pallas import tpu as pltpu
@@ -28,9 +29,9 @@
 
 
 def kernel(
-    hin, wq, wkv, wo, gain_in, cache, pages_in, cos_in, sin_in, length, owner,
+    hin, wq, wkv, wo, gain_in, cache, pages_in, inverse_in, owner_in, length,
     bout, pool,
-    gain, pages, cosv, sinv, bias, cachev, wq_l, wo_l, hA, part1, rbuf, ssend, srecv, sbuf2, qbuf, kvnew, S, msend, mixb, osend, ob, placed, obuf, pbuf,
+    owner, gain_raw, gain, pages, inverse, cosv, sinv, bias, cachev, wq_l, wo_l, hA, part1, rbuf, ssend, srecv, sbuf2, qbuf, kvnew, S, msend, mixb, osend, ob, placed, obuf, pbuf,
     insem, csem, h0s, h0r, h2s, h2r, wqs, wqr, wks, wkr, wos, wor,
     s1, r1, ss_s, ss_r, s2, r2, s3, r3, s4, r4, s5, r5, s6, r6, s7, r7, s7f, r7f, so, ro, ps, pr,
 ):
@@ -50,7 +51,7 @@
     def got(dst, rsem):
         pltpu.make_async_copy(dst, dst, rsem).wait()
 
-    inputs = ((gain_in, gain), (pages_in, pages), (cos_in, cosv), (sin_in, sinv))
+    inputs = ((gain_in, gain_raw), (pages_in, pages), (inverse_in, inverse), (owner_in, owner))
     for i, (src, dst) in enumerate(inputs):
         pltpu.make_async_copy(src, dst, insem.at[i]).start()
     cache_copy = pltpu.make_async_copy(cache, cachev, csem)
@@ -79,8 +80,85 @@
 
     own_dest = (c == own) & (k == u)
 
+    pl.semaphore_wait(barrier, 2 * (NCH - 1) + NSEC * NTP - 1 + 8 - own_dest.astype(jnp.int32))
+
+    def wq_copy(d):
+        peer = (y + d) % NSEC
+        src = wq.at[:, pl.ds(pl.multiple_of(peer * QC, QC), QC)]
+        dst = wq_l.at[y, :, pl.ds(0, QC)]
+        return lambda: remote(src, dst, wqs.at[d], wqr.at[y], (peer, c, t)), src, dst
+
+    def wkv_copy(d):
+        peer = (y + d) % NSEC
+        src = wkv.at[:, pl.ds(pl.multiple_of(peer * HD, HD), HD)]
+        dst = wq_l.at[y, :, pl.ds(QC, HD)]
+        return lambda: remote(src, dst, wks.at[d], wkr.at[y], (peer, c, t)), src, dst
+
+    def wo_copy(d):
+        peer = (y + d) % NSEC
+        src = wo.at[pl.ds(pl.multiple_of(peer * QC, QC), QC), :]
+        return lambda: remote(src, wo_l.at[k, y % 2], wos.at[d], wor.at[k, y % 2], (peer, c, 2 * u + y // 2)), src
+
+    def first_hop(st, d, far):
+        peer = (c + d) % NCH
+        src = hin.at[pl.ds(STREAMS[st][0], R), pl.ds(pl.multiple_of(peer * QC, QC), QC)]
+        dst = hA.at[st, t // 2, c, :, pl.ds(pl.multiple_of((t % 2) * QC, QC), QC)]
+        dev = (y, peer, across if far else t)
+        return lambda: remote(src, dst, h0s.at[st, far, d], h0r.at[st, far, c], dev), src, dst
+
+    def columns(st, tt):
+        return hA.at[st, tt // 2, :, :, pl.ds(pl.multiple_of((tt % 2) * QC, QC), QC)]
+
+    def second_hop(st, far):
+        piece = columns(st, across if far else t)
+        return remote(piece, piece, h2s.at[st, far], h2r.at[st, far], twin)
+
+    def first_sends(st):
+        _, src, dst = first_hop(st, 0, 0)
+        pltpu.make_async_copy(src, dst, h0r.at[st, 0, c]).start()
+        first_hop(st, 0, 1)[0]().start()
+        for d in range(1, NCH):
+            first_hop(st, d, 0)[0]().start()
+            first_hop(st, d, 1)[0]().start()
+
+    def second_sends(st):
+        for far in range(2):
+            tt = across if far else t
+            for d in range(NCH):
+                g = (c + NCH - d) % NCH
+                got(hA.at[st, tt // 2, g, :, pl.ds(pl.multiple_of((tt % 2) * QC, QC), QC)], h0r.at[st, far, g])
+            second_hop(st, far).start()
+
+    first_sends(0)
+    for d in range(1, NSEC):
+        wq_copy(d)[0]().start()
+        wkv_copy(d)[0]().start()
+    _, src, dst = wq_copy(0)
+    pltpu.make_async_copy(src, dst, wqr.at[y]).start()
+    _, src, dst = wkv_copy(0)
+    pltpu.make_async_copy(src, dst, wkr.at[y]).start()
+    for st in range(1, NS):
+        first_sends(st)
+    for d in range(NSEC):
+        if d:
+            wo_copy(d)[0]().start()
+        else:
+            @pl.when(k == y // 2)
+            def _():
+                pltpu.make_async_copy(wo_copy(0)[1], wo_l.at[k, y % 2], wor.at[k, y % 2]).start()
+
+            @pl.when(k != y // 2)
+            def _():
+                wo_copy(0)[0]().start()
+
     for i, (src, dst) in enumerate(inputs):
         pltpu.make_async_copy(src, dst, insem.at[i]).wait()
+    gain[...] = gain_raw[...].astype(F32)
+    row_pos = length[0] + lax.broadcasted_iota(jnp.int32, (NEW, HD), 0)
+    angles = row_pos.astype(F32) * inverse[...]
+    lane = lax.broadcasted_iota(jnp.int32, (NEW, HD), 1)
+    cosv[...] = jnp.cos(angles)
+    sinv[...] = jnp.where(lane < HD // 2, -1.0, 1.0) * jnp.sin(angles)
     n_pages = PREFIX // PAGE
     logical = lax.broadcasted_iota(jnp.int32, (8, n_pages), 1)
     live = jnp.clip(length[0] - logical * PAGE, 0, PAGE).astype(F32).astype(BF)
@@ -99,83 +177,13 @@
     row_in = lax.rem(lax.broadcasted_iota(jnp.int32, (NCHUNK, CH), 1), PAGE).astype(F32)
     bias[...] = jnp.where(row_in + 0.5 < count, 0.0, -1e30)
 
-    pl.semaphore_wait(barrier, 2 * (NCH - 1) + NSEC * NTP - 1 + 8 - own_dest.astype(jnp.int32))
-
-    def wq_copy(d):
-        peer = (y + d) % NSEC
-        src = wq.at[:, pl.ds(pl.multiple_of(peer * QC, QC), QC)]
-        dst = wq_l.at[y, :, pl.ds(0, QC)]
-        return lambda: remote(src, dst, wqs.at[d], wqr.at[y], (peer, c, t)), src, dst
-
-    def wkv_copy(d):
-        peer = (y + d) % NSEC
-        src = wkv.at[:, pl.ds(pl.multiple_of(peer * HD, HD), HD)]
-        dst = wq_l.at[y, :, pl.ds(QC, HD)]
-        return lambda: remote(src, dst, wks.at[d], wkr.at[y], (peer, c, t)), src, dst
-
-    def wo_copy(d):
-        peer = (y + d) % NSEC
-        src = wo.at[pl.ds(pl.multiple_of(peer * QC, QC), QC), :]
-        return lambda: remote(src, wo_l.at[k, y % 2], wos.at[d], wor.at[k, y % 2], (peer, c, 2 * u + y // 2)), src
-
-    def first_hop(st, d, far):
-        peer = (c + d) % NCH
-        src = hin.at[pl.ds(STREAMS[st][0], R), pl.ds(pl.multiple_of(peer * QC, QC), QC)]
-        dst = hA.at[st, t // 2, c, :, pl.ds(pl.multiple_of((t % 2) * QC, QC), QC)]
-        dev = (y, peer, across if far else t)
-        return lambda: remote(src, dst, h0s.at[st, far, d], h0r.at[st, far, c], dev), src, dst
-
-    def columns(st, tt):
-        return hA.at[st, tt // 2, :, :, pl.ds(pl.multiple_of((tt % 2) * QC, QC), QC)]
-
-    def second_hop(st, far):
-        piece = columns(st, across if far else t)
-        return remote(piece, piece, h2s.at[st, far], h2r.at[st, far], twin)
-
-    def first_sends(st):
-        _, src, dst = first_hop(st, 0, 0)
-        pltpu.make_async_copy(src, dst, h0r.at[st, 0, c]).start()
-        first_hop(st, 0, 1)[0]().start()
-        for d in range(1, NCH):
-            first_hop(st, d, 0)[0]().start()
-            first_hop(st, d, 1)[0]().start()
-
-    def second_sends(st):
-        for far in range(2):
-            tt = across if far else t
-            for d in range(NCH):
-                g = (c + NCH - d) % NCH
-                got(hA.at[st, tt // 2, g, :, pl.ds(pl.multiple_of((tt % 2) * QC, QC), QC)], h0r.at[st, far, g])
-            second_hop(st, far).start()
-
-    first_sends(0)
-    for d in range(1, NSEC):
-        wq_copy(d)[0]().start()
-        wkv_copy(d)[0]().start()
-    _, src, dst = wq_copy(0)
-    pltpu.make_async_copy(src, dst, wqr.at[y]).start()
-    _, src, dst = wkv_copy(0)
-    pltpu.make_async_copy(src, dst, wkr.at[y]).start()
-    for st in range(1, NS):
-        first_sends(st)
-    for d in range(NSEC):
-        if d:
-            wo_copy(d)[0]().start()
-        else:
-            @pl.when(k == y // 2)
-            def _():
-                pltpu.make_async_copy(wo_copy(0)[1], wo_l.at[k, y % 2], wor.at[k, y % 2]).start()
-
-            @pl.when(k != y // 2)
-            def _():
-                wo_copy(0)[0]().start()
-
     second_sends(0)
     for d in range(NSEC):
         g = (y + NSEC - d) % NSEC
         got(wq_l.at[g, :, pl.ds(0, QC)], wqr.at[g])
         got(wq_l.at[g, :, pl.ds(QC, HD)], wkr.at[g])
-        row = gain[pl.ds(g * NCH + c, 1), :]
+        halves = [gain[pl.ds((g * NCH + c) * 2 + a, 1), :] for a in range(2)]
+        row = jnp.concatenate(halves, axis=1)
         column = jnp.transpose(jnp.broadcast_to(row, (128, QC)))
         for a in range(PC // 128):
             part = wq_l[g, :, a * 128:(a + 1) * 128].astype(F32) * column
@@ -578,13 +586,9 @@
 
 
 def local(block_input, norm_gain, w_query, w_kv, w_out, kv_cache, page_table, prefix_len, page_owner):
-    length = prefix_len[0]
-    gain = norm_gain.astype(F32).reshape(NSEC * NCH, WIDTH // (NSEC * NCH))
-
-    lane = jnp.arange(HD)
-    inverse = 500000.0 ** (-((lane % (HD // 2)).astype(F32) * 2.0 / HD))
-    angles = (length + jnp.arange(NEW)).astype(F32)[:, None] * inverse[None, :]
-    sine = jnp.where(lane[None, :] < HD // 2, -1.0, 1.0) * jnp.sin(angles)
+    lane = np.arange(HD, dtype=np.float64)[None, :] % (HD // 2)
+    inverse = jnp.asarray((500000.0 ** (-(lane * 2.0 / HD))).astype(np.float32))
+
     vm = pl.BlockSpec(memory_space=pltpu.VMEM)
     hbm = pl.BlockSpec(memory_space=pltpu.HBM)
     dma = pltpu.SemaphoreType.DMA
@@ -595,11 +599,14 @@
             jax.ShapeDtypeStruct((NEW, WIDTH // NTP), BF),
             jax.ShapeDtypeStruct((NSEC, 2 * PAGE, 512), BF),
         ),
-        in_specs=[hbm] * 9 + [pl.BlockSpec(memory_space=pltpu.SMEM)] * 2,
+        in_specs=[hbm] * 9 + [pl.BlockSpec(memory_space=pltpu.SMEM)],
         out_specs=(vm, vm),
         scratch_shapes=[
-            V((NSEC * NCH, QC), F32),
+            pltpu.SMEM((NEW // PAGE,), jnp.int32),
+            V((WIDTH // 128, 128), BF),
+            V((WIDTH // 128, 128), F32),
             V((1, PREFIX // PAGE), jnp.int32),
+            V((1, HD), F32),
             V((NEW, HD), F32),
             V((NEW, HD), F32),
             V((NCHUNK, CH), F32),
@@ -641,11 +648,17 @@
             dma((NSEC,)), dma((NSEC,)),
         ],
         compiler_params=pltpu.CompilerParams(
-            collective_id=0, has_side_effects=True, vmem_limit_bytes=56 * 1024 * 1024
+            collective_id=0, has_side_effects=True, vmem_limit_bytes=32 * 1024 * 1024
         ),
     )(
-        block_input[0], w_query, w_kv, w_out, gain, kv_cache.reshape(PREFIX, 512), page_table,
-        jnp.cos(angles), sine, prefix_len, page_owner[0, :, 0],
+        *[
+            pltpu.with_memory_space_constraint(v, pltpu.HBM)
+            for v in (
+                block_input[0], w_query, w_kv, w_out, norm_gain.reshape(WIDTH // 128, 128),
+                kv_cache.reshape(PREFIX, 512), page_table, inverse, page_owner[0, :, 0],
+            )
+        ],
+        prefix_len,
     )
     return bout[None, None], pool.reshape(1, 1, 2 * NSEC, PAGE, 512)
 

time: 177 us -> 171 us (0.966)
  local copies, waits for them, and re-layouts: 4.58 us -> 1.36 us
    unnamed x2, local copies, waits for them, and re-layouts: 3.24 us -> 1.36 us
where the time goes in v4:
time: 171 us
  Pallas kernels  169 us (99%)
    pallas_call x1, Pallas kernels, local(): pl.pallas_call(kernel, out_shape=(jax.ShapeDtypeStruct((NEW, WIDTH // NTP...  169 us

profile of v4, /device:TPU:25, one launch (start us, length us, event | category | flops | bytes accessed | tf_op | source)
XLA Modules:
  0.0 171.2 jit_solution(10632164133928897044)
XLA Ops:
  1.3 168.5 %shard_map.113 = (bf16[64,2048]{1,0:T(8,128)(2,1)S(1)}, bf16[4,32,512]{2,1,0:T(8,128)(2,1)S(1)}) custom-call(bf16[64,2048]{1,0:T(8,128)(2,1)} %bitcast.9, bf16[256,1024]{1,0:T(8,128)(2,1)} %wq.1, bf16[256,512]{1,0:T(8,128)(2,1)} %wkv.1, bf16[1024,256]{1,0:T(8,128)(2,1)} %wo.1, bf16[64,128]{1,0:T(8,128)(2,1)} %bitcast.10, bf16[4096,512]{1,0:T(8,128)(2,1)} %bitcast.8, ...), custom_call_target="tpu_custom_call" | custom-call | tf_op jit(solution)/shard_map/pallas_call | solution.py:596
  169.8 0.7 copy.15
  170.5 0.7 copy.16

commit v5 on v4

--- a/solution.py
+++ b/solution.py
@@ -28,6 +28,18 @@
 F32 = jnp.float32
 
 
+NEAR_CHAIN = ((0, 0), (2, 1), (2, 0), (1, 1), (3, 1), (1, 0), (3, 0), (0, 1))
+NEAR_SECTION = ((0, 0), (2, 1), (1, 1), (3, 1), (2, 0), (0, 1), (1, 0), (3, 0))
+
+
+def there(i, d, steps):
+    return (i // 2 + steps[d][0]) % 4 * 2 + (i % 2 + steps[d][1]) % 2
+
+
+def back(i, d, steps):
+    return (i // 2 + 4 - steps[d][0]) % 4 * 2 + (i % 2 + steps[d][1]) % 2
+
+
 def kernel(
     hin, wq, wkv, wo, gain_in, cache, pages_in, inverse_in, owner_in, length,
     bout, pool,
@@ -61,8 +73,8 @@
 
     barrier = pltpu.get_barrier_semaphore()
     for d in range(1, NCH):
-        pl.semaphore_signal(barrier, inc=1, device_id=(y, (c + d) % NCH, t), device_id_type=MESH)
-        pl.semaphore_signal(barrier, inc=1, device_id=(y, (c + d) % NCH, across), device_id_type=MESH)
+        pl.semaphore_signal(barrier, inc=1, device_id=(y, there(c, d, NEAR_CHAIN), t), device_id_type=MESH)
+        pl.semaphore_signal(barrier, inc=1, device_id=(y, there(c, d, NEAR_CHAIN), across), device_id_type=MESH)
     for dy in range(NSEC):
         for dt in range(NTP):
             if dy or dt:
@@ -100,7 +112,7 @@
         return lambda: remote(src, wo_l.at[k, y % 2], wos.at[d], wor.at[k, y % 2], (peer, c, 2 * u + y // 2)), src
 
     def first_hop(st, d, far):
-        peer = (c + d) % NCH
+        peer = there(c, d, NEAR_CHAIN)
         src = hin.at[pl.ds(STREAMS[st][0], R), pl.ds(pl.multiple_of(peer * QC, QC), QC)]
         dst = hA.at[st, t // 2, c, :, pl.ds(pl.multiple_of((t % 2) * QC, QC), QC)]
         dev = (y, peer, across if far else t)
@@ -125,7 +137,7 @@
         for far in range(2):
             tt = across if far else t
             for d in range(NCH):
-                g = (c + NCH - d) % NCH
+                g = back(c, d, NEAR_CHAIN)
                 got(hA.at[st, tt // 2, g, :, pl.ds(pl.multiple_of((tt % 2) * QC, QC), QC)], h0r.at[st, far, g])
             second_hop(st, far).start()
 
@@ -209,12 +221,12 @@
         cache_copy.wait()
 
     def ag_copy(st, e):
-        g = (own + e) % 8
+        g = there(own, e, NEAR_SECTION)
         piece = hA.at[st, k, own]
         return remote(piece, piece, s7.at[st, e], r7.at[st, own], (g // 2, c, 2 * (g % 2) + k))
 
     def twin_copy(st, e):
-        g = (own + 8 - e) % 8
+        g = back(own, e, NEAR_SECTION)
         piece = hA.at[st, k, g]
         return remote(piece, piece, s7f.at[st, e], r7f.at[st, g], twin)
 
@@ -223,23 +235,19 @@
             ag_copy(st, e).start()
         twin_copy(st, 0).start()
 
-    def ag_forward(st, s):
-        @pl.when(s < NSEC - 1)
+    def ag_wait(st, s):
+        @pl.when(s == 0)
+        def _():
+            first_wait(st)
+
+        @pl.when(s > 0)
         def _():
             for e in range(1, 8):
-                g = (own + 8 - e) % 8
+                g = back(own, e, NEAR_SECTION)
                 got(hA.at[st, k, g], r7.at[st, g])
                 twin_copy(st, e).start()
-
-    def ag_wait(st, s):
-        @pl.when(s == 0)
-        def _():
-            first_wait(st)
-
-        @pl.when(s > 0)
-        def _():
             for e in range(8):
-                g = (own + 8 - e) % 8
+                g = back(own, e, NEAR_SECTION)
                 got(hA.at[st, 1 - k, g], r7f.at[st, g])
 
     def ag_sent(st):
@@ -249,11 +257,11 @@
             twin_copy(st, e).wait_send()
 
     def p1_copy(st, d):
-        peer = (c + d) % NCH
+        peer = there(c, d, NEAR_CHAIN)
         return remote(part1.at[st, peer], rbuf.at[st, c], s1.at[st, d], r1.at[st, c], (y, peer, t))
 
     def ss_copy(st, d):
-        peer = (c + d) % NCH
+        peer = there(c, d, NEAR_CHAIN)
         return remote(ssend.at[st, peer], srecv.at[st, c], ss_s.at[st, d], ss_r.at[st, c], (y, peer, t))
 
     def project(st, s):
@@ -293,7 +301,7 @@
     def finish_projection(st, s):
         r0 = STREAMS[st][0]
         for d in range(1, NCH):
-            g = (c + NCH - d) % NCH
+            g = back(c, d, NEAR_CHAIN)
             got(rbuf.at[st, g], r1.at[st, g])
             got(srecv.at[st, g], ss_r.at[st, g])
         total = rbuf[st, 0].astype(F32)
@@ -423,12 +431,12 @@
             p2_copy(st, s).wait_send()
 
     def p4_copy(st, d):
-        peer = (c + d) % NCH
+        peer = there(c, d, NEAR_CHAIN)
         piece = mixb.at[st, k, c]
         return remote(piece, piece, s4.at[st, d], r4.at[st, c], (y, peer, t))
 
     def p5_copy(st, d):
-        g = (c + NCH - d) % NCH
+        g = back(c, d, NEAR_CHAIN)
         piece = mixb.at[st, k, g]
         return remote(piece, piece, s5.at[st, d], r5.at[st, g], twin)
 
@@ -447,12 +455,12 @@
 
     def spread_twin(st, s):
         for d in range(1, NCH):
-            g = (c + NCH - d) % NCH
+            g = back(c, d, NEAR_CHAIN)
             got(mixb.at[st, k, g], r4.at[st, g])
             p5_copy(st, d).start()
 
     def p6_copy(st, e):
-        g = (own + e) % 8
+        g = there(own, e, NEAR_SECTION)
         return remote(osend.at[st, g], ob.at[st, own], s6.at[st, e], r6.at[st, own], (g // 2, c, 2 * (g % 2) + k))
 
     def bout_copy(st, s, a):
@@ -498,7 +506,7 @@
 
     def output_projection(st, s):
         for d in range(NCH):
-            g = (c + NCH - d) % NCH
+            g = back(c, d, NEAR_CHAIN)
             got(mixb.at[st, 1 - k, g], r5.at[st, g])
         if st == 0:
             @pl.when(s == 0)
@@ -534,7 +542,7 @@
 
     def residual(st, s):
         for e in range(1, 8):
-            g = (own + 8 - e) % 8
+            g = back(own, e, NEAR_SECTION)
             got(ob.at[st, g], r6.at[st, g])
         total = ob[st, 0].astype(F32)
         for g in range(1, 8):
@@ -556,10 +564,12 @@
         mix(st, s)
         spread(st, s)
 
+    def twin_and_output(st, s):
+        spread_twin(st, s)
+        output_projection(st, s)
+
     def section_step(s, carry):
-        for phase in (
-            project, finish_projection, attend_and_spread, spread_twin, output_projection, residual, ag_forward
-        ):
+        for phase in (project, finish_projection, attend_and_spread, twin_and_output, residual):
             for st in range(NS):
                 phase(st, s)
         return carry
@@ -569,7 +579,7 @@
     for st in range(NS):
         bout_sent(st, NSEC - 1)
         for d in range(NCH):
-            g = (c + d) % NCH
+            g = there(c, d, NEAR_CHAIN)
             mine = (y == c // 2) & (c == g) & (t == 2 * (c % 2) + t // 2)
 
             @pl.when(jnp.logical_not(mine))

time: 171 us -> 156 us (0.912)
  Pallas kernels: 169 us -> 153 us
    pallas_call x1, Pallas kernels: 169 us -> 153 us  [local(): pl.pallas_call(kernel, out_shape=(jax.ShapeDtypeStruct((NEW, WIDTH // NTP...]
where the time goes in v5:
time: 156 us
  Pallas kernels  153 us (98%)
    pallas_call x1, Pallas kernels, local(): pl.pallas_call(kernel, out_shape=(jax.ShapeDtypeStruct((NEW, WIDTH // NTP...  153 us

profile of v5, /device:TPU:25, one launch (start us, length us, event | category | flops | bytes accessed | tf_op | source)
XLA Modules:
  0.0 156.0 jit_solution(8647227221450525994)
XLA Ops:
  1.3 153.3 %shard_map.113 = (bf16[64,2048]{1,0:T(8,128)(2,1)S(1)}, bf16[4,32,512]{2,1,0:T(8,128)(2,1)S(1)}) custom-call(bf16[64,2048]{1,0:T(8,128)(2,1)} %bitcast.9, bf16[256,1024]{1,0:T(8,128)(2,1)} %wq.1, bf16[256,512]{1,0:T(8,128)(2,1)} %wkv.1, bf16[1024,256]{1,0:T(8,128)(2,1)} %wo.1, bf16[64,128]{1,0:T(8,128)(2,1)} %bitcast.10, bf16[4096,512]{1,0:T(8,128)(2,1)} %bitcast.8, ...), custom_call_target="tpu_custom_call" | custom-call | tf_op jit(solution)/shard_map/pallas_call | solution.py:606
  154.6 0.7 copy.15
  155.3 0.7 copy.16

commit v6 on v5

--- a/solution.py
+++ b/solution.py
@@ -29,7 +29,7 @@
 
 
 NEAR_CHAIN = ((0, 0), (2, 1), (2, 0), (1, 1), (3, 1), (1, 0), (3, 0), (0, 1))
-NEAR_SECTION = ((0, 0), (2, 1), (1, 1), (3, 1), (2, 0), (0, 1), (1, 0), (3, 0))
+NEAR_SECTION = ((0, 0), (2, 1), (2, 0), (1, 1), (3, 1), (0, 1), (1, 0), (3, 0))
 
 
 def there(i, d, steps):
@@ -142,7 +142,7 @@
             second_hop(st, far).start()
 
     first_sends(0)
-    for d in range(1, NSEC):
+    for d in (2, 1, 3):
         wq_copy(d)[0]().start()
         wkv_copy(d)[0]().start()
     _, src, dst = wq_copy(0)
@@ -151,7 +151,7 @@
     pltpu.make_async_copy(src, dst, wkr.at[y]).start()
     for st in range(1, NS):
         first_sends(st)
-    for d in range(NSEC):
+    for d in (2, 1, 3, 0):
         if d:
             wo_copy(d)[0]().start()
         else:
@@ -266,15 +266,22 @@
 
     def project(st, s):
         ag_wait(st, s)
-        total = None
-        for half in range(2):
-            x = hA[st, half].reshape(NCH * R, 512)
-            w = wq_l[pl.ds(2 * half, 2)].reshape(512, PC)
-            term = jnp.dot(x, w, preferred_element_type=F32)
-            total = term if total is None else total + term
-        part1[st] = total.astype(BF).reshape(NCH, R, PC)
-        for d in range(1, NCH):
-            p1_copy(st, d).start()
+        z = c // 2
+        for group in ((2,), (1, 3, 0)):
+            total = None
+            for half in range(2):
+                x = jnp.concatenate(
+                    [hA[st, half, pl.ds((z + dz) % 4 * 2, 2)].reshape(2 * R, 512) for dz in group], axis=0
+                )
+                w = wq_l[pl.ds(2 * half, 2)].reshape(512, PC)
+                term = jnp.dot(x, w, preferred_element_type=F32)
+                total = term if total is None else total + term
+            for i, dz in enumerate(group):
+                piece = total[i * 2 * R:(i + 1) * 2 * R].astype(BF).reshape(2, R, PC)
+                part1[st, pl.ds((z + dz) % 4 * 2, 2)] = piece
+            if len(group) == 1:
+                for d in (1, 2):
+                    p1_copy(st, d).start()
         ones = jnp.ones((8, 128), BF)
         for g in range(NCH):
             acc = None
@@ -291,6 +298,8 @@
             row = row + lax.dot_general(ones, low, dims, preferred_element_type=F32)
             ssend[st, g] = jnp.concatenate([row, jnp.zeros((8, 128 - R), F32)], axis=1)
         for d in range(1, NCH):
+            if d > 2:
+                p1_copy(st, d).start()
             ss_copy(st, d).start()
         rbuf[st, c] = part1[st, c]
         srecv[st, c] = ssend[st, c]
@@ -513,16 +522,20 @@
             def _():
                 wo_wait()
 
-        for b in range(2):
-            total = None
-            for a in range(2):
-                x = mixb[st, a].reshape(NCH * R, QC)
-                term = jnp.dot(x, wo_l[a, b], preferred_element_type=F32)
-                total = term if total is None else total + term
-            osend[st, :, :, b * QC:(b + 1) * QC] = total.astype(BF).reshape(NCH, R, QC)
-
-        for e in range(1, 8):
-            p6_copy(st, e).start()
+        for group in ((2,), (1, 3, 0)):
+            for b in range(2):
+                total = None
+                for a in range(2):
+                    x = jnp.concatenate(
+                        [mixb[st, a, pl.ds((y + dy) % 4 * 2, 2)].reshape(2 * R, QC) for dy in group], axis=0
+                    )
+                    term = jnp.dot(x, wo_l[a, b], preferred_element_type=F32)
+                    total = term if total is None else total + term
+                for i, dy in enumerate(group):
+                    piece = total[i * 2 * R:(i + 1) * 2 * R].astype(BF).reshape(2, R, QC)
+                    osend[st, pl.ds((y + dy) % 4 * 2, 2), :, b * QC:(b + 1) * QC] = piece
+            for e in range(1, 3) if len(group) == 1 else range(3, 8):
+                p6_copy(st, e).start()
         ob[st, own] = osend[st, own]
         for d in range(1, NCH):
             p4_copy(st, d).wait_send()

time: 156 us -> 155 us (level)
  no operation moved by 1% of the time
where the time goes in v6:
time: 155 us; the launch traced here: 154 us
  Pallas kernels  152 us (98%)
    pallas_call x1, Pallas kernels, local(): pl.pallas_call(kernel, out_shape=(jax.ShapeDtypeStruct((NEW, WIDTH // NTP...  152 us

profile of v6, /device:TPU:25, one launch (start us, length us, event | category | flops | bytes accessed | tf_op | source)
XLA Modules:
  0.0 154.4 jit_solution(829349715223592860)
XLA Ops:
  1.3 151.8 %shard_map.113 = (bf16[64,2048]{1,0:T(8,128)(2,1)S(1)}, bf16[4,32,512]{2,1,0:T(8,128)(2,1)S(1)}) custom-call(bf16[64,2048]{1,0:T(8,128)(2,1)} %bitcast.9, bf16[256,1024]{1,0:T(8,128)(2,1)} %wq.1, bf16[256,512]{1,0:T(8,128)(2,1)} %wkv.1, bf16[1024,256]{1,0:T(8,128)(2,1)} %wo.1, bf16[64,128]{1,0:T(8,128)(2,1)} %bitcast.10, bf16[4096,512]{1,0:T(8,128)(2,1)} %bitcast.8, ...), custom_call_target="tpu_custom_call" | custom-call | tf_op jit(solution)/shard_map/pallas_call | solution.py:619
  153.1 0.7 copy.15
  153.8 0.7 copy.16

commit v7 on v6

--- a/solution.py
+++ b/solution.py
@@ -189,7 +189,8 @@
     row_in = lax.rem(lax.broadcasted_iota(jnp.int32, (NCHUNK, CH), 1), PAGE).astype(F32)
     bias[...] = jnp.where(row_in + 0.5 < count, 0.0, -1e30)
 
-    second_sends(0)
+    for st in range(NS):
+        second_sends(st)
     for d in range(NSEC):
         g = (y + NSEC - d) % NSEC
         got(wq_l.at[g, :, pl.ds(0, QC)], wqr.at[g])
@@ -200,9 +201,6 @@
         for a in range(PC // 128):
             part = wq_l[g, :, a * 128:(a + 1) * 128].astype(F32) * column
             wq_l[g, :, a * 128:(a + 1) * 128] = part.astype(BF)
-    for st in range(1, NS):
-        second_sends(st)
-
     def first_wait(st):
         got(columns(st, 2 * u + 1 - k), h2r.at[st, 0])
         got(columns(st, across_twin), h2r.at[st, 1])
@@ -235,7 +233,7 @@
             ag_copy(st, e).start()
         twin_copy(st, 0).start()
 
-    def ag_wait(st, s):
+    def ag_forward(st, s):
         @pl.when(s == 0)
         def _():
             first_wait(st)
@@ -246,6 +244,10 @@
                 g = back(own, e, NEAR_SECTION)
                 got(hA.at[st, k, g], r7.at[st, g])
                 twin_copy(st, e).start()
+
+    def ag_wait(st, s):
+        @pl.when(s > 0)
+        def _():
             for e in range(8):
                 g = back(own, e, NEAR_SECTION)
                 got(hA.at[st, 1 - k, g], r7f.at[st, g])
@@ -264,18 +266,31 @@
         peer = there(c, d, NEAR_CHAIN)
         return remote(ssend.at[st, peer], srecv.at[st, c], ss_s.at[st, d], ss_r.at[st, c], (y, peer, t))
 
+    def rows_of(ref, st, half, base, group, width):
+        parts = [ref[st, half, pl.ds((base + step) % 4 * 2, 2)].reshape(2 * R, width) for step in group]
+        return jnp.concatenate(parts, axis=0)
+
+    def squares_of(st, half):
+        sums = []
+        for g in range(NCH):
+            wide = hA[st, half, g].astype(F32)
+            square = wide * wide
+            sums.append(sum(square[:, a * 128:(a + 1) * 128] for a in range(1, 4)) + square[:, :128])
+        return sums
+
     def project(st, s):
+        z = c // 2
+        ag_forward(st, s)
+        w_own = wq_l[pl.ds(2 * k, 2)].reshape(512, PC)
+        before = jnp.dot(rows_of(hA, st, k, z, (2, 1, 3, 0), 512), w_own, preferred_element_type=F32)
+        own_squares = squares_of(st, k)
         ag_wait(st, s)
-        z = c // 2
+        w_other = wq_l[pl.ds(2 - 2 * k, 2)].reshape(512, PC)
+        done = 0
         for group in ((2,), (1, 3, 0)):
-            total = None
-            for half in range(2):
-                x = jnp.concatenate(
-                    [hA[st, half, pl.ds((z + dz) % 4 * 2, 2)].reshape(2 * R, 512) for dz in group], axis=0
-                )
-                w = wq_l[pl.ds(2 * half, 2)].reshape(512, PC)
-                term = jnp.dot(x, w, preferred_element_type=F32)
-                total = term if total is None else total + term
+            x = rows_of(hA, st, 1 - k, z, group, 512)
+            total = before[done:done + x.shape[0]] + jnp.dot(x, w_other, preferred_element_type=F32)
+            done += x.shape[0]
             for i, dz in enumerate(group):
                 piece = total[i * 2 * R:(i + 1) * 2 * R].astype(BF).reshape(2, R, PC)
                 part1[st, pl.ds((z + dz) % 4 * 2, 2)] = piece
@@ -283,14 +298,8 @@
                 for d in (1, 2):
                     p1_copy(st, d).start()
         ones = jnp.ones((8, 128), BF)
-        for g in range(NCH):
-            acc = None
-            for half in range(2):
-                wide = hA[st, half, g].astype(F32)
-                square = wide * wide
-                for a in range(4):
-                    piece = square[:, a * 128:(a + 1) * 128]
-                    acc = piece if acc is None else acc + piece
+        for g, (mine, other) in enumerate(zip(own_squares, squares_of(st, 1 - k))):
+            acc = mine + other
             high = acc.astype(BF)
             low = (acc - high.astype(F32)).astype(BF)
             dims = (((1,), (1,)), ((), ()))
@@ -514,26 +523,26 @@
                     wo_copy(0)[0]().wait_send()
 
     def output_projection(st, s):
+        if st == 0:
+            @pl.when(s == 0)
+            def _():
+                wo_wait()
+
+        x_own = rows_of(mixb, st, k, y, (2, 1, 3, 0), QC)
+        before = [jnp.dot(x_own, wo_l[k, b], preferred_element_type=F32) for b in range(2)]
         for d in range(NCH):
             g = back(c, d, NEAR_CHAIN)
             got(mixb.at[st, 1 - k, g], r5.at[st, g])
-        if st == 0:
-            @pl.when(s == 0)
-            def _():
-                wo_wait()
-
+        done = 0
         for group in ((2,), (1, 3, 0)):
+            x = rows_of(mixb, st, 1 - k, y, group, QC)
             for b in range(2):
-                total = None
-                for a in range(2):
-                    x = jnp.concatenate(
-                        [mixb[st, a, pl.ds((y + dy) % 4 * 2, 2)].reshape(2 * R, QC) for dy in group], axis=0
-                    )
-                    term = jnp.dot(x, wo_l[a, b], preferred_element_type=F32)
-                    total = term if total is None else total + term
+                total = before[b][done:done + x.shape[0]]
+                total = total + jnp.dot(x, wo_l[1 - k, b], preferred_element_type=F32)
                 for i, dy in enumerate(group):
                     piece = total[i * 2 * R:(i + 1) * 2 * R].astype(BF).reshape(2, R, QC)
                     osend[st, pl.ds((y + dy) % 4 * 2, 2), :, b * QC:(b + 1) * QC] = piece
+            done += x.shape[0]
             for e in range(1, 3) if len(group) == 1 else range(3, 8):
                 p6_copy(st, e).start()
         ob[st, own] = osend[st, own]

time: 155 us -> 154 us (level)
  no operation moved by 1% of the time
where the time goes in v7:
time: 154 us
  Pallas kernels  151 us (98%)
    pallas_call x1, Pallas kernels, local(): pl.pallas_call(kernel, out_shape=(jax.ShapeDtypeStruct((NEW, WIDTH // NTP...  151 us

profile of v7, /device:TPU:25, one launch (start us, length us, event | category | flops | bytes accessed | tf_op | source)
XLA Modules:
  0.0 154.0 jit_solution(12958990735957388347)
XLA Ops:
  1.3 151.4 %shard_map.113 = (bf16[64,2048]{1,0:T(8,128)(2,1)S(1)}, bf16[4,32,512]{2,1,0:T(8,128)(2,1)S(1)}) custom-call(bf16[64,2048]{1,0:T(8,128)(2,1)} %bitcast.9, bf16[256,1024]{1,0:T(8,128)(2,1)} %wq.1, bf16[256,512]{1,0:T(8,128)(2,1)} %wkv.1, bf16[1024,256]{1,0:T(8,128)(2,1)} %wo.1, bf16[64,128]{1,0:T(8,128)(2,1)} %bitcast.10, bf16[4096,512]{1,0:T(8,128)(2,1)} %bitcast.8, ...), custom_call_target="tpu_custom_call" | custom-call | tf_op jit(solution)/shard_map/pallas_call | solution.py:628
  152.7 0.7 copy.15
  153.4 0.7 copy.16
